TPU v7x, 512 devices: a whole 4x4x16 slice. The times are simulated.
512 devices in a mesh: seq: 16 (over z), exp: 32 (over y, x, core).
Axes of the slice: x: 4, y: 4, z: 16, core: 2. Of those that a mesh axis runs over, the one named last changes fastest.
Arguments:
- adjoint: bfloat16 [2048, 2880], P('seq'), may hold values from -6 to 6
- seed_grad: float32 [2048, 2880], P('seq', 'exp'), may hold values from -3 to 3
- layer_input: bfloat16 [2048, 2880], P('seq'), may hold values from -6 to 6
- norm_gain: float32 [2880], replicated, may hold values from 0.5 to 1.5
- router_weight: bfloat16 [2880, 32], replicated, may hold values from -0.109375 to 0.109375
- routes: int32 [2048, 4], P('seq'), may hold values from 0 to 31, all different within a row; in each aligned block of 128 rows (0 to 127, 128 to 255, ...) at most 32 rows name the same one
- expert_out: bfloat16 [2048, 4, 2880], P('seq', None, 'exp'), may hold values from -6 to 6
- stored_query: bfloat16 [2048, 2048], P('seq', 'exp'), may hold values from -3 to 3
- stored_key: bfloat16 [2048, 256], P('seq'), may hold values from -3 to 3
- stored_value: bfloat16 [2048, 256], P('seq'), may hold values from -6 to 6
- query_weight: bfloat16 [2880, 2048], P(None, 'exp'), may hold values from -0.109375 to 0.109375
- key_weight: bfloat16 [2880, 256], P('exp'), may hold values from -0.109375 to 0.109375
- value_weight: bfloat16 [2880, 256], P('exp'), may hold values from -0.109375 to 0.109375
- output_weight: bfloat16 [2048, 2880], P('exp'), may hold values from -0.125 to 0.125
- gate_weight: bfloat16 [32, 2880, 1536], P('exp', None, 'seq'), may hold values from -0.109375 to 0.109375
- up_weight: bfloat16 [32, 2880, 1536], P('exp', None, 'seq'), may hold values from -0.109375 to 0.109375
- down_weight: bfloat16 [32, 1536, 2880], P('exp', 'seq'), may hold values from -0.15625 to 0.15625
- stored_gate: bfloat16 [32, 512, 1536], P('exp', None, 'seq'), may hold values from -8 to 8
- stored_up: bfloat16 [32, 512, 1536], P('exp', None, 'seq'), may hold values from -6 to 6
Outputs:
- new_adjoint: float32 [2048, 2880], P('seq', 'exp')
Inputs may be any that keep to these rules, and one draw needn't show every extreme that they name: `routes`: in each block of 128 consecutive tokens every expert is named by at most 32 tokens, and some block names some expert 32 times.
All inputs are finite; a program needn't handle non-finite values.
Results may differ from a plain program's by a relative error of at most 0.019.
Values may be sent and summed in bfloat16 or wider, within the bound.
No kernel may reach another device: no remote copies, remote signals or barrier semaphores. Data moves between devices by JAX's collectives and lax.ppermute only.
A program may use at most 64 MiB of HBM per device.

v0:
```python
import jax
import jax.numpy as jnp
from jax import lax
from jax.sharding import PartitionSpec as P

HEAD_DIM = 64
WINDOW = 128
QH = 32
KVH = 4


EPSILON = 1e-05
PRECISE = lax.Precision.HIGHEST


def padded(value, sides, width):
    for axis, dim in sides:
        count, length = (lax.axis_size(axis), value.shape[dim])
        up = [(i, (i + 1) % count) for i in range(count - 1)]
        down = [(j, i) for i, j in up]
        last = lax.slice_in_dim(value, length - width, length, axis=dim)
        first = lax.slice_in_dim(value, 0, width, axis=dim)
        before = lax.ppermute(last, axis, up)
        after = lax.ppermute(first, axis, down)
        value = jnp.concatenate([before, value, after], axis=dim)
    return value


def norm_parts(layer_input, norm_gain):
    values = layer_input.astype(jnp.float32)
    inverse = lax.rsqrt(jnp.mean(values * values, axis=-1, keepdims=True) + EPSILON)
    return (values, inverse, values * inverse * norm_gain)


def on_device(
    adjoint,
    seed_grad,
    layer_input,
    norm_gain,
    router_weight,
    routes,
    expert_out,
    stored_query,
    stored_key,
    stored_value,
    query_weight,
    key_weight,
    value_weight,
    output_weight,
    gate_weight,
    up_weight,
    down_weight,
    stored_gate,
    stored_up,
):
    tok_here = adjoint.shape[0]
    features = adjoint.shape[1]
    experts = router_weight.shape[1]
    seq_count = lax.axis_size("seq")
    position = lax.axis_index("exp")
    block = lax.axis_index("seq")
    capacity = stored_gate.shape[1] // seq_count
    cols_dev = seed_grad.shape[1]
    first_col = position * cols_dev
    values, inverse, normed = norm_parts(layer_input, norm_gain)
    logits = jnp.dot(normed.astype(jnp.bfloat16), router_weight, preferred_element_type=jnp.float32)
    picked = (routes[:, :, None] == lax.broadcasted_iota(jnp.int32, (1, 1, experts), 2)).astype(
        jnp.float32
    )
    chosen = jnp.sum(picked * logits[:, None, :], axis=2)
    raised = jnp.exp(chosen)
    shares = raised / jnp.sum(raised, axis=1, keepdims=True)
    adjoint_float = adjoint.astype(jnp.float32)
    adjoint_cols = lax.dynamic_slice_in_dim(adjoint_float, first_col, cols_dev, 1)
    aligned_part = jnp.sum(adjoint_cols[:, None, :] * expert_out.astype(jnp.float32), axis=2)
    logit_back = shares * (aligned_part - jnp.sum(shares * aligned_part, axis=1, keepdims=True))
    coef_rows = jnp.sum(logit_back[:, :, None] * picked, axis=1)
    router_part = jnp.dot(coef_rows, router_weight.astype(jnp.float32).T, precision=PRECISE)
    route_gate = shares.astype(jnp.bfloat16)
    named = routes == position
    named_count = jnp.sum(named.astype(jnp.int32), axis=1)
    gate_mine = jnp.sum(jnp.where(named, route_gate.astype(jnp.float32), 0.0), axis=1)
    slot_rank = jnp.cumsum(named_count) - named_count
    slot_index = jnp.where(named_count > 0, slot_rank, -1)
    placing = (slot_index[:, None] == lax.broadcasted_iota(jnp.int32, (1, capacity), 1)).astype(
        jnp.bfloat16
    )
    scaled = (gate_mine[:, None] * adjoint_float).astype(jnp.bfloat16)
    expert_input = jnp.einsum(
        "ls,ld->sd", placing, scaled, preferred_element_type=jnp.float32
    ).astype(jnp.bfloat16)
    joined = jnp.concatenate([gate_weight[0], up_weight[0]], axis=1)
    down_local = down_weight[0]
    gate_store = stored_gate[0]
    up_store = stored_up[0]
    gate_here = gate_store.astype(jnp.float32)
    up_here = up_store.astype(jnp.float32)
    hidden_back = jnp.einsum(
        "nd,fd->nf",
        lax.all_gather(expert_input, "seq", axis=0, tiled=True),
        down_local,
        preferred_element_type=jnp.float32,
    )
    sigma = jax.nn.sigmoid(gate_here)
    gate_back = (hidden_back * up_here * (sigma * (1.0 + gate_here * (1.0 - sigma)))).astype(
        jnp.bfloat16
    )
    up_back = (hidden_back * (gate_here * sigma)).astype(jnp.bfloat16)
    both_backs = jnp.concatenate([gate_back, up_back], axis=1)
    band_terms = jnp.einsum("nf,df->nd", both_backs, joined, preferred_element_type=jnp.float32)
    returned = lax.all_to_all(
        band_terms.astype(jnp.bfloat16).reshape(seq_count, capacity, features),
        "seq",
        split_axis=0,
        concat_axis=0,
        tiled=True,
    )
    results = jnp.sum(returned.astype(jnp.float32), axis=0)
    moe_part = jnp.dot(placing.astype(jnp.float32), results, precision=PRECISE)
    heads_here = query_weight.shape[1] // HEAD_DIM
    group_size = QH // KVH
    kv_width = stored_key.shape[1]
    score_scale = HEAD_DIM ** (-0.5)
    rim = WINDOW - 1
    packs = []
    local_head = 0
    head_index = position * heads_here + local_head
    kv_start = head_index // group_size * HEAD_DIM
    out_back = jnp.einsum(
        "ld,ed->le", adjoint, output_weight, preferred_element_type=jnp.float32
    ).astype(jnp.bfloat16)
    packs.append(stored_query)
    packs.append(lax.dynamic_slice_in_dim(stored_key, kv_start, HEAD_DIM, 1))
    packs.append(lax.dynamic_slice_in_dim(stored_value, kv_start, HEAD_DIM, 1))
    packs.append(out_back)
    packed = jnp.concatenate(packs, axis=1)
    extended = padded(packed, (("seq", 0),), rim)
    total_len = seq_count * tok_here
    query_pos = block * tok_here + lax.broadcasted_iota(jnp.int32, (tok_here + rim, 1), 0)
    key_pos = block * tok_here - rim + lax.broadcasted_iota(jnp.int32, (1, tok_here + 2 * rim), 1)
    row_valid = query_pos < total_len
    visible = (query_pos >= key_pos) & (query_pos - key_pos < WINDOW) & (key_pos >= 0) & row_valid
    kv_back = jnp.zeros((tok_here, 2 * kv_width), jnp.float32)
    local_head = 0
    head_index = position * heads_here + local_head
    kv_start = head_index // group_size * HEAD_DIM
    base = local_head * 4 * HEAD_DIM
    query_ext = extended[:, base : base + HEAD_DIM]
    key_ext = extended[:, base + HEAD_DIM : base + 2 * HEAD_DIM]
    value_ext = extended[:, base + 2 * HEAD_DIM : base + 3 * HEAD_DIM]
    out_ext = extended[:, base + 3 * HEAD_DIM : base + 4 * HEAD_DIM]
    query_rows = query_ext[rim:]
    out_rows = out_ext[rim:]
    scores = (
        jnp.einsum("qe,ke->qk", query_rows, key_ext, preferred_element_type=jnp.float32)
        * score_scale
    )
    raised_scores = jnp.where(visible, jnp.exp(scores), 0.0)
    row_total = jnp.sum(raised_scores, axis=1, keepdims=True)
    soft_rows = raised_scores / jnp.where(row_valid, row_total, 1.0)
    soft_own = soft_rows[:, rim : rim + tok_here]
    value_grad = jnp.einsum(
        "qk,qe->ke", soft_own.astype(jnp.bfloat16), out_rows, preferred_element_type=jnp.float32
    ).astype(jnp.bfloat16)
    attn_back = jnp.einsum("qe,ke->qk", out_rows, value_ext, preferred_element_type=jnp.float32)
    score_back = (
        soft_rows * (attn_back - jnp.sum(soft_rows * attn_back, axis=1, keepdims=True))
    ).astype(jnp.bfloat16)
    query_grad = (
        jnp.einsum("qk,ke->qe", score_back[:tok_here], key_ext, preferred_element_type=jnp.float32)
        * score_scale
    ).astype(jnp.bfloat16)
    key_grad = (
        jnp.einsum(
            "qk,qe->ke",
            score_back[:, rim : rim + tok_here],
            query_rows,
            preferred_element_type=jnp.float32,
        )
        * score_scale
    ).astype(jnp.bfloat16)
    head_sum = jnp.einsum("lf,df->ld", query_grad, query_weight, preferred_element_type=jnp.float32)
    kv_back = lax.dynamic_update_slice_in_dim(kv_back, key_grad.astype(jnp.float32), kv_start, 1)
    value_now = lax.dynamic_slice_in_dim(kv_back, kv_width + kv_start, HEAD_DIM, 1)
    kv_back = lax.dynamic_update_slice_in_dim(
        kv_back, value_now + value_grad.astype(jnp.float32), kv_width + kv_start, 1
    )
    kv_rows = jnp.concatenate([key_weight, value_weight], axis=1).astype(jnp.float32)
    gain_cols = lax.dynamic_slice_in_dim(norm_gain, first_col, cols_dev, 0)
    values_cols = lax.dynamic_slice_in_dim(values, first_col, cols_dev, 1)
    norm_part = jnp.dot(values_cols * gain_cols, kv_rows, precision=PRECISE)
    partial_value = router_part + moe_part + head_sum
    summed, kv_all, norm_all = (
        lax.psum(partial_value.astype(jnp.bfloat16), "exp").astype(jnp.float32),
        lax.psum(kv_back.astype(jnp.bfloat16), "exp").astype(jnp.float32),
        lax.psum(norm_part.astype(jnp.bfloat16), "exp").astype(jnp.float32),
    )
    summed_cols = lax.dynamic_slice_in_dim(summed, first_col, cols_dev, 1)
    row_stat = jnp.sum(values * norm_gain * summed, axis=-1, keepdims=True)
    projected = jnp.dot(kv_all, kv_rows.T, precision=PRECISE)
    lifted_cols = gain_cols * (summed_cols + projected)
    mean_term = (row_stat + jnp.sum(kv_all * norm_all, axis=-1, keepdims=True)) / features
    return seed_grad + adjoint_cols + inverse * lifted_cols - values_cols * inverse**3 * mean_term


def solution(mesh):
    placed = (
        P("seq", None),
        P("seq", "exp"),
        P("seq", None),
        P(),
        P(),
        P("seq", None),
        P("seq", None, "exp"),
        P("seq", "exp"),
        P("seq", None),
        P("seq", None),
        P(None, "exp"),
        P("exp", None),
        P("exp", None),
        P("exp", None),
        P("exp", None, "seq"),
        P("exp", None, "seq"),
        P("exp", "seq", None),
        P("exp", None, "seq"),
        P("exp", None, "seq"),
    )
    return jax.shard_map(
        on_device, mesh=mesh, in_specs=placed, out_specs=P("seq", "exp"), check_vma=False
    )
```

profile of v0, /device:TPU:1, one launch (start us, length us, event | category | flops | bytes accessed | tf_op | source)
XLA Modules:
  0.0 390.4 jit_solution(5410020309994831307)
XLA Ops:
  6.6 1.3 convert_element_type.96
  7.9 0.4 multiply_reduce_fusion.1
  8.3 0.6 multiply_multiply_fusion
  8.9 0.5 convert_reduce_fusion.1
  9.5 1.5 fusion.17
  11.2 0.2 reduce-window.8
  11.5 1.0 multiply_reduce_fusion.4
  12.5 1.2 multiply_reduce_fusion.5
  13.7 1.2 convolution_convert_fusion.1
  14.9 72.6 %all-gather.2.cloned.1.call-done = bf16[512,2880]{1,0:T(8,128)(2,1)} async-done(((bf16[32,2880]{1,0:T(8,128)(2,1)}), bf16[512,2880]{1,0:T(8,128)(2,1)}) %all-gather.2.cloned.1.call-update) | async-done | bytes 2949136 | tf_op jit(solution)/shard_map/all_gather | solution.py:100
  87.5 3.0 fusion.33
  90.6 1.0 convolution_convert_fusion
  91.6 3.0 copy.36
  94.6 7.0 %all-to-all-start = ((bf16[16,32,2880]{2,1,0:T(8,128)(2,1)}), bf16[16,32,2880]{2,1,0:T(8,128)(2,1)}, u32[]{:S(2)}, u32[]{:S(2)}) async-start(bf16[16,32,2880]{2,1,0:T(8,128)(2,1)} %bitcast.31), calls=%async_computation | async-start | bytes 6029312 | tf_op jit(solution)/shard_map/all_to_all | solution.py:111
  102.1 0.3 convolution_convert_fusion.3
  102.5 1.3 collective-permute-start
  103.8 4.0 %collective-permute-start.1 = (bf16[127,256]{0,1:T(8,128)(2,1)S(1)}, bf16[127,256]{0,1:T(8,128)(2,1)S(1)}, u32[]{:S(2)}, u32[]{:S(2)}) collective-permute-start(bf16[127,256]{0,1:T(8,128)(2,1)S(1)} %get-tuple-element.16), channel_id=1, source_target_pairs={{0,32},{32,64},{64,96},{96,128},{128,160},{160,192},{192,224},{224... | collective-permute-start | bytes 195080 | tf_op jit(solution)/shard_map/ppermute | solution.py:23
  108.2 1.0 convolution_convert_fusion.2
  109.2 124.1 %collective-permute-done = bf16[127,256]{0,1:T(8,128)(2,1)S(1)} collective-permute-done((bf16[127,256]{0,1:T(8,128)(2,1)S(1)}, bf16[127,256]{0,1:T(8,128)(2,1)S(1)}, u32[]{:S(2)}, u32[]{:S(2)}) %collective-permute-start) | collective-permute-done | bytes 65056 | tf_op jit(solution)/shard_map/ppermute | solution.py:24
  233.5 0.4 fusion.59
  233.8 0.4 multiply_reduce_fusion.2
  234.4 0.2 fusion.14
  234.6 0.2 add_dynamic-update-slice_fusion
  234.8 0.7 convert_element_type.122
  235.5 1.5 fusion.16
  237.0 2.3 convert_reduce_fusion
  239.4 1.4 fusion.42
  240.8 1.9 fusion.1
  242.7 137.3 %all-reduce.3.cloned.1.call-done = (bf16[128,512]{0,1:T(8,128)(2,1)}, bf16[128,2880]{0,1:T(8,128)(2,1)}, bf16[128,512]{0,1:T(8,128)(2,1)}) async-done(((bf16[128,512]{0,1:T(8,128)(2,1)}, bf16[128,2880]{0,1:T(8,128)(2,1)}, bf16[128,512]{0,1:T(8,128)(2,1)}), (bf16[128,512]{0,1:T(8,128)(2,1)}, bf16[128,2880]{0,1:T(8,128)(2,1)}, bf16[128,512]{0,1:T(8,128)(2,1)})) %all-reduce.3.cloned.1.call-update) | async-done | bytes 999440 | tf_op jit(solution)/shard_map/psum | solution.py:195
  380.0 1.3 convert_element_type.117
  381.3 0.5 multiply_reduce_fusion
  381.9 1.6 fusion.10
  (108 shorter events, 1.6 us)
Async XLA Ops:
  6.5 81.0 %copy-start = (bf16[1,96,2880]{2,1,0:T(8,128)(2,1)S(1)}, bf16[1,96,2880]{2,1,0:T(8,128)(2,1)}, u32[]{:S(2)}) copy-start(bf16[1,96,2880]{2,1,0:T(8,128)(2,1)} %param.35) | copy-start | bytes 1658884
  6.5 81.0 %all-gather.2.cloned.1.call-start = ((), (), s32[]{:S(2)}) async-start(), calls=%async_computation.1 | async-start | bytes 3203072 | tf_op jit(solution)/shard_map/all_gather | solution.py:100
  6.5 2.4 copy-start.21
  6.5 2.9 copy-start.25
  7.9 7.0 %copy-start.6 = (f32[128,2880]{0,1:T(8,128)}, f32[128,2880]{0,1:T(8,128)S(1)}, u32[]{:S(2)}) copy-start(f32[128,2880]{0,1:T(8,128)S(1)} %convert_element_type.96) | copy-start | bytes 4423684
  7.9 5.8 %copy-start.1 = (bf16[128,2880]{0,1:T(8,128)(2,1)S(1)}, bf16[128,2880]{0,1:T(8,128)(2,1)}, u32[]{:S(2)}) copy-start(bf16[128,2880]{0,1:T(8,128)(2,1)} %param.19) | copy-start | bytes 2211844
  11.0 76.5 %copy-start.35 = (bf16[1,512,96]{1,2,0:T(8,128)(2,1)S(1)}, bf16[1,512,96]{1,2,0:T(8,128)(2,1)}, u32[]{:S(2)}) copy-start(bf16[1,512,96]{1,2,0:T(8,128)(2,1)} %param.37) | copy-start | bytes 294916
  11.0 76.5 %copy-start.36 = (bf16[1,512,96]{1,2,0:T(8,128)(2,1)S(1)}, bf16[1,512,96]{1,2,0:T(8,128)(2,1)}, u32[]{:S(2)}) copy-start(bf16[1,512,96]{1,2,0:T(8,128)(2,1)} %param.36) | copy-start | bytes 294916
  11.1 79.5 %copy-start.27 = (f32[128]{0:T(128)}, f32[128]{0:T(128)S(1)}, u32[]{:S(2)}) copy-start(f32[128]{0:T(128)S(1)} %exponential_reduce_fusion) | copy-start | bytes 1540
  11.5 79.1 %copy-start.30 = (s32[128]{0:T(128)}, s32[128]{0:T(128)S(1)}, u32[]{:S(2)}) copy-start(s32[128]{0:T(128)S(1)} %compare_select_fusion) | copy-start | bytes 1540
  87.5 3.0 copy-start.8
  87.5 3.0 copy-start.9
  94.6 7.1 %copy-start.23 = (bf16[128,256]{1,0:T(8,128)(2,1)S(1)}, bf16[128,256]{1,0:T(8,128)(2,1)}, u32[]{:S(2)}) copy-start(bf16[128,256]{1,0:T(8,128)(2,1)} %param.28) | copy-start | bytes 196612
  94.6 7.1 %copy-start.24 = (bf16[128,256]{1,0:T(8,128)(2,1)S(1)}, bf16[128,256]{1,0:T(8,128)(2,1)}, u32[]{:S(2)}) copy-start(bf16[128,256]{1,0:T(8,128)(2,1)} %param.27) | copy-start | bytes 196612
  94.6 7.4 %copy-start.2 = (bf16[128,2880]{0,1:T(8,128)(2,1)S(1)}, bf16[128,2880]{0,1:T(8,128)(2,1)}, u32[]{:S(2)}) copy-start(bf16[128,2880]{0,1:T(8,128)(2,1)} %param.19) | copy-start | bytes 2211844
  94.6 7.4 %copy-start.13 = (bf16[64,2880]{1,0:T(8,128)(2,1)S(1)}, bf16[64,2880]{1,0:T(8,128)(2,1)}, u32[]{:S(2)}) copy-start(bf16[64,2880]{1,0:T(8,128)(2,1)} %param.32) | copy-start | bytes 1105924
  94.6 7.7 %copy-start.14 = (bf16[128,64]{0,1:T(8,128)(2,1)S(1)}, bf16[128,64]{0,1:T(8,128)(2,1)}, u32[]{:S(2)}) copy-start(bf16[128,64]{0,1:T(8,128)(2,1)} %param.26) | copy-start | bytes 49156
  94.6 142.4 %all-to-all-start = ((bf16[16,32,2880]{2,1,0:T(8,128)(2,1)}), bf16[16,32,2880]{2,1,0:T(8,128)(2,1)}, u32[]{:S(2)}, u32[]{:S(2)}) async-start(bf16[16,32,2880]{2,1,0:T(8,128)(2,1)} %bitcast.31), calls=%async_computation | async-start | bytes 6029312 | tf_op jit(solution)/shard_map/all_to_all | solution.py:111
  101.6 6.2 %copy-start.4 = (bf16[128,2880]{0,1:T(8,128)(2,1)S(1)}, bf16[128,2880]{0,1:T(8,128)(2,1)}, u32[]{:S(2)}) copy-start(bf16[128,2880]{0,1:T(8,128)(2,1)} %param.21) | copy-start | bytes 2211844
  101.6 278.3 %all-reduce.3.cloned.1.call-start = ((), (), s32[]{:S(2)}) async-start(), calls=%async_computation.2 | async-start | bytes 1998848 | tf_op jit(solution)/shard_map/psum | solution.py:195
  102.0 5.8 %copy-start.11 = (bf16[128,64]{0,1:T(8,128)(2,1)}, bf16[128,64]{0,1:T(8,128)(2,1)S(1)}, u32[]{:S(2)}) copy-start(bf16[128,64]{0,1:T(8,128)(2,1)S(1)} %copy.41) | copy-start | bytes 49156
  102.3 5.6 %copy-start.26 = (f32[2880]{0:T(1024)S(1)}, f32[2880]{0:T(1024)}, u32[]{:S(2)}) copy-start(f32[2880]{0:T(1024)} %param.22) | copy-start | bytes 34564
  102.3 5.7 %copy-start.19 = (bf16[90,256]{1,0:T(8,128)(2,1)S(1)}, bf16[90,256]{1,0:T(8,128)(2,1)}, u32[]{:S(2)}) copy-start(bf16[90,256]{1,0:T(8,128)(2,1)} %param.30) | copy-start | bytes 138244
  102.4 5.7 %copy-start.20 = (bf16[90,256]{1,0:T(8,128)(2,1)S(1)}, bf16[90,256]{1,0:T(8,128)(2,1)}, u32[]{:S(2)}) copy-start(bf16[90,256]{1,0:T(8,128)(2,1)} %param.31) | copy-start | bytes 138244
  102.4 5.8 %copy-start.28 = (f32[128]{0:T(128)S(1)}, f32[128]{0:T(128)}, u32[]{:S(2)}) copy-start(f32[128]{0:T(128)} %copy-done.27) | copy-start | bytes 1540
  102.4 5.8 %copy-start.29 = (f32[128]{0:T(128)S(1)}, f32[128]{0:T(128)}, u32[]{:S(2)}) copy-start(f32[128]{0:T(128)} %get-tuple-element.5) | copy-start | bytes 1540
  102.4 5.8 %copy-start.22 = (s32[128,4]{0,1:T(4,128)S(1)}, s32[128,4]{0,1:T(4,128)}, u32[]{:S(2)}) copy-start(s32[128,4]{0,1:T(4,128)} %param.24) | copy-start | bytes 6148
  102.4 130.9 %copy-start.15 = (bf16[128,64]{0,1:T(8,128)(2,1)S(1)}, bf16[128,64]{0,1:T(8,128)(2,1)}, u32[]{:S(2)}) copy-start(bf16[128,64]{0,1:T(8,128)(2,1)} %param.26) | copy-start | bytes 49156
  102.5 130.8 %collective-permute-start = (bf16[127,256]{0,1:T(8,128)(2,1)S(1)}, bf16[127,256]{0,1:T(8,128)(2,1)S(1)}, u32[]{:S(2)}, u32[]{:S(2)}) collective-permute-start(bf16[127,256]{0,1:T(8,128)(2,1)S(1)} %get-tuple-element.17), channel_id=1, source_target_pairs={{32,0},{64,32},{96,64},{128,96},{160,128},{192,160},{224,192},{256... | collective-permute-start | bytes 195080 | tf_op jit(solution)/shard_map/ppermute | solution.py:24
  103.8 129.5 %collective-permute-start.1 = (bf16[127,256]{0,1:T(8,128)(2,1)S(1)}, bf16[127,256]{0,1:T(8,128)(2,1)S(1)}, u32[]{:S(2)}, u32[]{:S(2)}) collective-permute-start(bf16[127,256]{0,1:T(8,128)(2,1)S(1)} %get-tuple-element.16), channel_id=1, source_target_pairs={{0,32},{32,64},{64,96},{96,128},{128,160},{160,192},{192,224},{224... | collective-permute-start | bytes 195080 | tf_op jit(solution)/shard_map/ppermute | solution.py:23
  107.8 125.5 %copy-start.12 = (bf16[128,64]{0,1:T(8,128)(2,1)S(1)}, bf16[128,64]{0,1:T(8,128)(2,1)}, u32[]{:S(2)}) copy-start(bf16[128,64]{0,1:T(8,128)(2,1)} %copy-done.11) | copy-start | bytes 49156
  108.0 126.3 %copy-start.7 = (f32[128,2880]{0,1:T(8,128)}, f32[128,2880]{0,1:T(8,128)S(1)}, u32[]{:S(2)}) copy-start(f32[128,2880]{0,1:T(8,128)S(1)} %convert_element_type.97) | copy-start | bytes 4423684
  (10 other events, 16.4 us)
Sparse Core Ops, SparseCore 0:
  15.0 72.4 all-gather.1
  242.8 137.1 all-reduce.2
where the time goes:
time: 391 us; the launch traced here: 390 us
  waiting for transfers between devices  334 us (85%)
  matrix products  15.5 us (4%)
  between operations  14 us (4%)
  starting transfers between devices  12.3 us (3%)
  other arithmetic  10.6 us (3%)
    psum x1, waiting for transfers between devices, on_device(): lax.psum(kv_back.astype(jnp.bfloat16), 'exp').astype(jnp.float32)  137 us
    ppermute x1, waiting for transfers between devices, padded(): after = lax.ppermute(first, axis, down)  124 us
    all_gather x1, waiting for transfers between devices, on_device(): lax.all_gather(expert_input, 'seq', axis=0, tiled=True)  72.6 us
  transfers between devices with their start and end apart: 5, of which 3 were waited for; matrix products, arithmetic and copies ran while one was open for 1% of the time, Pallas kernels for 0%

commit v1 on v0

v1 whole, which is shorter than its diff:
```python
import jax
import jax.numpy as jnp
from jax import lax
from jax.experimental import pallas as pl
from jax.experimental.pallas import tpu as pltpu
from jax.sharding import Mesh
from jax.sharding import PartitionSpec as P

D = 2880
HEAD_DIM = 64
WINDOW = 128
QH = 32
KVH = 4
TOPK = 4
EXPERTS = 32
CAP = 32
TOK = 128
BAND = 96
HALF = BAND // 2
COLS = D // 32
PART = 96
SENDERS = D // PART
BLOCKS = 8
MINE = BLOCKS * CAP
EPSILON = 1e-05
SCALE = HEAD_DIM ** (-0.5)

BF = jnp.bfloat16
F32 = jnp.float32
SEQ = ("zh", "zl")


def dot(left, right, contract=((1,), (0,))):
    return lax.dot_general(left, right, (contract, ((), ())), preferred_element_type=F32)


def rows_of(shape):
    return lax.broadcasted_iota(jnp.int32, shape, 0)


def lanes_of(shape):
    return lax.broadcasted_iota(jnp.int32, shape, 1)


def split(value):
    high = value.astype(BF)
    return high, (value - high.astype(F32)).astype(BF)


def whole(shape_dtypes, flops=0, moved=0):
    return dict(
        out_shape=[jax.ShapeDtypeStruct(s, d) for s, d in shape_dtypes],
        compiler_params=pltpu.CompilerParams(vmem_limit_bytes=40 * 1024 * 1024),
        cost_estimate=pl.CostEstimate(flops=flops, bytes_accessed=moved, transcendentals=0),
    )


SMEM = pl.BlockSpec(memory_space=pltpu.SMEM)
VMEM = pl.BlockSpec(memory_space=pltpu.VMEM)


def route_kernel(where, layer, gain, router, routes, adjoint, out_w, pay, inverse, shares, out_back):
    values = layer[...].astype(F32)
    inv = lax.rsqrt(jnp.sum(values * values, axis=0, keepdims=True) / D + EPSILON)
    inverse[...] = inv
    high, low = split(router[...].astype(F32) * gain[...])
    logits = (dot(high, layer[...]) + dot(low, layer[...])) * inv
    names = rows_of((EXPERTS, TOK))
    picked = [names == routes[k : k + 1, :] for k in range(TOPK)]
    raised = [
        jnp.exp(jnp.sum(jnp.where(p, logits, 0.0), axis=0, keepdims=True)) for p in picked
    ]
    total = raised[0] + raised[1] + raised[2] + raised[3]
    taken = sum(p.astype(F32) for p in picked)
    earlier = (rows_of((TOK, TOK)) < lanes_of((TOK, TOK))).astype(BF)
    ranks = dot(taken.astype(BF), earlier)
    line = rows_of((16, TOK))
    meta = jnp.zeros((16, TOK), F32)
    for k in range(TOPK):
        share = raised[k] / total
        shares[k : k + 1, :] = share
        rank = jnp.sum(jnp.where(picked[k], ranks, 0.0), axis=0, keepdims=True)
        meta = jnp.where(line == k, routes[k : k + 1, :].astype(F32), meta)
        meta = jnp.where(line == TOPK + k, rank, meta)
        meta = jnp.where(line == 2 * TOPK + k, share, meta)
    start = pl.multiple_of(jnp.minimum(where[0], SENDERS - 1) * PART, PART)
    pay[0:PART, :] = adjoint[pl.ds(start, PART), :]
    pay[PART:, :] = meta.astype(BF)
    out_back[...] = dot(out_w[...], adjoint[...]).astype(BF)


def pack_kernel(where, down, gate, up, store_g, store_u, query_w, to_next, to_prev, own_g, own_u, query_parts):
    def chosen(parity):
        i, j = rows_of((16 * CAP, MINE)), lanes_of((16 * CAP, MINE))
        return (i == (2 * (j // CAP) + parity) * CAP + j % CAP).astype(BF)

    parity = where[1]
    here, there = chosen(parity), chosen(1 - parity)
    own_g[...] = dot(store_g[...], here).astype(BF)
    own_u[...] = dot(store_u[...], here).astype(BF)
    sent_g = dot(store_g[...], there).astype(BF)
    sent_u = dot(store_u[...], there).astype(BF)
    for first, ref in ((HALF, to_next), (0, to_prev)):
        for n, weight in enumerate((down, gate, up)):
            ref[n * HALF : (n + 1) * HALF, :] = weight[first : first + HALF, :]
        ref[3 * HALF :, :] = jnp.zeros((16, D), BF)
        for n, sent in enumerate((sent_g, sent_u)):
            for m in range(3):
                lane = (3 * n + m) * MINE
                ref[3 * HALF :, lane : lane + MINE] = sent[first + 16 * m : first + 16 * m + 16, :]
    for c in range(32):
        piece = query_w[:, c * COLS : (c + 1) * COLS]
        query_parts[c, :, :] = jnp.zeros((32, 256), BF)
        query_parts[c, :, 0:COLS] = piece[0:32]
        query_parts[c, :, 128 : 128 + COLS] = piece[32:64]


def attend_kernel(where, query, out_back, kv, kv_prev, next_q, aligned, grads):
    block = where[2]
    key_at, query_at = rows_of((TOK, TOK)), lanes_of((TOK, TOK))
    same = key_at <= query_at
    before = key_at > query_at

    def rows(q, out, before_kv, same_kv, before_mask):
        def half(kv_rows, mask):
            scores = dot(kv_rows[:, :HEAD_DIM], q) * SCALE
            return jnp.where(mask, jnp.exp(scores), 0.0), dot(kv_rows[:, HEAD_DIM:], out)

        p_before, a_before = half(before_kv, before_mask)
        p_same, a_same = half(same_kv, same)
        total = jnp.sum(p_before, axis=0, keepdims=True) + jnp.sum(p_same, axis=0, keepdims=True)
        p_before, p_same = p_before / total, p_same / total
        mean = jnp.sum(p_before * a_before, axis=0, keepdims=True) + jnp.sum(
            p_same * a_same, axis=0, keepdims=True
        )
        return (
            p_before.astype(BF),
            (p_before * (a_before - mean)).astype(BF),
            p_same.astype(BF),
            (p_same * (a_same - mean)).astype(BF),
        )

    q, out = query[...], out_back[...]
    own, prev, following = kv[...], kv_prev[...], next_q[TOK:, :]
    q_next, out_next = next_q[0:HEAD_DIM, :], next_q[HEAD_DIM : 2 * HEAD_DIM, :]
    _, sb_prev, p_own, sb_own = rows(q, out, prev, own, before & (block > 0))
    p_next, sb_next, _, _ = rows(q_next, out_next, own, following, before)
    live = jnp.where(block < 15, 1.0, 0.0)
    over = ((0,), (0,))
    across = ((1,), (1,))
    grads[0:64, :] = (
        (dot(prev[:, :HEAD_DIM], sb_prev, over) + dot(own[:, :HEAD_DIM], sb_own, over)) * SCALE
    ).astype(BF)
    grads[64:128, :] = (
        (dot(q, sb_own, across) + live * dot(q_next, sb_next, across)) * SCALE
    ).astype(BF)
    grads[128:192, :] = (dot(out, p_own, across) + live * dot(out_next, p_next, across)).astype(BF)
    line = rows_of((16, TOK))
    tail = jnp.zeros((16, TOK), F32)
    for k in range(TOPK):
        high = aligned[k : k + 1, :].astype(BF).astype(F32)
        tail = jnp.where(line == k, high, tail)
        tail = jnp.where(line == TOPK + k, aligned[k : k + 1, :] - high, tail)
    grads[192:208, :] = tail.astype(BF)


def dispatch_kernel(gathered, query_parts, sent, places, gates):
    names = rows_of((EXPERTS, TOK)).astype(F32)
    for b in range(BLOCKS):
        meta = gathered[b, PART:, :].astype(F32)
        place = jnp.full((EXPERTS, TOK), -1.0, F32)
        gate = jnp.zeros((EXPERTS, TOK), F32)
        for k in range(TOPK):
            match = names == meta[k : k + 1, :]
            place = jnp.where(match, meta[TOPK + k : TOPK + k + 1, :] + CAP * (b % 4), place)
            gate = jnp.where(match, meta[2 * TOPK + k : 2 * TOPK + k + 1, :], gate)
        places[:, b * TOK : (b + 1) * TOK] = place
        gates[:, b * TOK : (b + 1) * TOK] = gate
    features = [
        jnp.concatenate([gathered[b, 0:PART, :] for b in range(4 * h, 4 * h + 4)], axis=1)
        for h in range(2)
    ]
    slot = rows_of((TOK, 4 * TOK)).astype(F32)

    def step(e, carry):
        for h in range(2):
            lanes = slice(h * 4 * TOK, (h + 1) * 4 * TOK)
            placing = jnp.where(
                slot == places[pl.ds(e, 1), lanes], gates[pl.ds(e, 1), lanes], 0.0
            ).astype(BF)
            sent[e, 0:PART, h * TOK : (h + 1) * TOK] = dot(
                features[h], placing, ((1,), (1,))
            ).astype(BF)
        return carry

    lax.fori_loop(0, EXPERTS, step, 0)
    sent[:, PART:, :] = query_parts[...]


def expert_kernel(rows, down, gate, up, own_g, own_u, from_prev, from_next, sent, total):
    features = rows[0:SENDERS, 0:PART, :].reshape(D, MINE)

    def act(hidden, g, u):
        g, u = g.astype(F32), u.astype(F32)
        sigma = jax.nn.sigmoid(g)
        return (
            (hidden * u * (sigma * (1.0 + g * (1.0 - sigma)))).astype(BF),
            (hidden * (g * sigma)).astype(BF),
        )

    def stored(ref, n):
        return jnp.concatenate(
            [ref[3 * HALF :, (3 * n + m) * MINE : (3 * n + m + 1) * MINE] for m in range(3)], axis=0
        )

    backs = list(act(dot(down[...], features), own_g[...], own_u[...]))
    for ref in (from_prev, from_next):
        backs += list(act(dot(ref[0:HALF, :], features), stored(ref, 0), stored(ref, 1)))
    weights = [gate[...], up[...]]
    for ref in (from_prev, from_next):
        weights += [ref[HALF : 2 * HALF, :], ref[2 * HALF : 3 * HALF, :]]
    total[0:D, :] = dot(
        jnp.concatenate(weights, axis=0), jnp.concatenate(backs, axis=0), ((0,), (0,))
    )
    total[D:, :] = jnp.zeros((8, MINE), F32)
    for c in range(32):
        sent[c, :, :] = total[c * COLS : c * COLS + PART, :].astype(BF)


def combine_kernel(returned, places, sent):
    slot = rows_of((TOK, 4 * TOK)).astype(F32)

    for h in range(2):
        lanes = slice(h * 4 * TOK, (h + 1) * 4 * TOK)

        def step(i, total):
            picks, terms = [], []
            for n in range(2):
                e = 2 * i + n
                picks.append((slot == places[pl.ds(e, 1), lanes]).astype(BF))
                terms.append(returned[e, :, h * TOK : (h + 1) * TOK])
            return total + dot(jnp.concatenate(terms, axis=1), jnp.concatenate(picks, axis=0))

        total = lax.fori_loop(0, EXPERTS // 2, step, jnp.zeros((PART, 4 * TOK), F32))
        for b in range(4):
            sent[4 * h + b, :, :] = total[:, b * TOK : (b + 1) * TOK].astype(BF)


def project_kernel(grads, rows, key_w, value_w, router, shares, routes, attended):
    total = jnp.zeros((PART, TOK), F32)
    for h in range(QH):
        for n in range(2):
            weight = rows[h, PART:, n * 128 : n * 128 + PART]
            total = total + dot(weight, grads[h, 32 * n : 32 * n + 32, :], ((0,), (0,)))
    group = QH // KVH
    for first, weight in ((64, key_w), (128, value_w)):
        sums = []
        for g in range(KVH):
            some = grads[g * group, first : first + 64, :].astype(F32)
            for h in range(g * group + 1, (g + 1) * group):
                some = some + grads[h, first : first + 64, :].astype(F32)
            sums.append(some)
        high, low = split(jnp.concatenate(sums, axis=0))
        total = total + dot(weight[...], high) + dot(weight[...], low)
    tail = grads[0, 192:208, :].astype(F32)
    for h in range(1, QH):
        tail = tail + grads[h, 192:208, :].astype(F32)
    aligned = [tail[k : k + 1, :] + tail[TOPK + k : TOPK + k + 1, :] for k in range(TOPK)]
    mean = sum(shares[k : k + 1, :] * aligned[k] for k in range(TOPK))
    names = rows_of((EXPERTS, TOK))
    coef = jnp.zeros((EXPERTS, TOK), F32)
    for k in range(TOPK):
        back = shares[k : k + 1, :] * (aligned[k] - mean)
        coef = jnp.where(names == routes[k : k + 1, :], back, coef)
    high, low = split(coef)
    attended[...] = total + dot(router[...], high) + dot(router[...], low)


def lift_kernel(bands, attended, gain, values, lifted, stat):
    total = attended[...]
    for b in range(BLOCKS):
        total = total + bands[b, :, :].astype(F32)
    total = jnp.where(rows_of((PART, TOK)) < COLS, total, 0.0) * gain[...]
    lifted[...] = total
    stat[...] = jnp.broadcast_to(
        jnp.sum(values[...] * total, axis=0, keepdims=True), (32, TOK)
    )


def finish_kernel(stats, lifted, values, inverse, base, result):
    mean = jnp.sum(stats[...], axis=0, keepdims=True) / D
    inv = inverse[...]
    result[...] = base[...] + (
        inv * lifted[0:COLS, :] - values[0:COLS, :] * (inv * inv * inv * mean)
    )


def on_device(
    adjoint,
    seed_grad,
    layer_input,
    norm_gain,
    router_weight,
    routes,
    expert_out,
    stored_query,
    stored_key,
    stored_value,
    query_weight,
    key_weight,
    value_weight,
    output_weight,
    gate_weight,
    up_weight,
    down_weight,
    stored_gate,
    stored_up,
):
    col = lax.axis_index("exp")
    block = lax.axis_index(SEQ)
    parity = lax.axis_index("zl")
    where = jnp.stack([col, parity, block]).astype(jnp.int32)
    first = col * COLS
    adjoint_t, layer_t, routes_t = adjoint.T, layer_input.T, routes.T
    to_next = [(i, (i + 1) % 16) for i in range(16)]
    to_prev = [(j, i) for i, j in to_next]

    pay, inverse, shares, out_back = pl.pallas_call(
        route_kernel,
        in_specs=[SMEM] + [VMEM] * 6,
        out_specs=[VMEM] * 4,
        **whole([((PART + 16, TOK), BF), ((1, TOK), F32), ((TOPK, TOK), F32), ((HEAD_DIM, TOK), BF)]),
        name="route",
    )(where, layer_t, norm_gain[None, :], router_weight.T, routes_t, adjoint_t, output_weight)
    gathered = lax.all_to_all(
        jnp.broadcast_to(pay[None], (BLOCKS, PART + 16, TOK)), "zh", 0, 0, tiled=True
    )

    kv_start = col // (QH // KVH) * HEAD_DIM
    kv = jnp.concatenate(
        [lax.dynamic_slice_in_dim(a, kv_start, HEAD_DIM, 1) for a in (stored_key, stored_value)], axis=1
    )
    query_t = stored_query.T
    kv_prev = lax.ppermute(kv, SEQ, to_next)
    from_next_q = lax.ppermute(jnp.concatenate([query_t, out_back, kv], axis=0), SEQ, to_prev)

    down, gate, up = down_weight[0], gate_weight[0].T, up_weight[0].T
    wide, narrow = ((3 * HALF + 16, D), BF), ((BAND, MINE), BF)
    w_next, w_prev, own_g, own_u, query_parts = pl.pallas_call(
        pack_kernel,
        in_specs=[SMEM] + [VMEM] * 6,
        out_specs=[VMEM] * 5,
        **whole([wide, wide, narrow, narrow, ((32, 32, 256), BF)]),
        name="pack",
    )(where, down, gate, up, stored_gate[0].T, stored_up[0].T, query_weight.T)
    w_from_prev = lax.ppermute(w_next, SEQ, to_next)
    w_from_next = lax.ppermute(w_prev, SEQ, to_prev)

    adjoint_cols = lax.dynamic_slice_in_dim(adjoint_t, first, COLS, 0).astype(F32)
    values = lax.dynamic_slice_in_dim(layer_t, first, COLS, 0).astype(F32)
    aligned = jnp.sum(adjoint_cols[:, None, :] * expert_out.transpose(2, 1, 0).astype(F32), axis=0)
    (grads,) = pl.pallas_call(
        attend_kernel,
        in_specs=[SMEM] + [VMEM] * 6,
        out_specs=[VMEM],
        **whole([((208, TOK), BF)]),
        name="attend",
    )(where, query_t, out_back, kv, kv_prev, from_next_q, aligned)
    all_grads = lax.all_gather(grads, "exp", axis=0)

    sent, places, _ = pl.pallas_call(
        dispatch_kernel,
        in_specs=[VMEM] * 2,
        out_specs=[VMEM] * 3,
        **whole([((32, PART + 32, MINE), BF), ((EXPERTS, BLOCKS * TOK), F32), ((EXPERTS, BLOCKS * TOK), F32)]),
        name="dispatch",
    )(gathered, query_parts)
    rows = lax.all_to_all(sent, "exp", 0, 0, tiled=True)
    (terms,) = pl.pallas_call(
        expert_kernel,
        in_specs=[VMEM] * 8,
        out_specs=[VMEM],
        scratch_shapes=[pltpu.VMEM((D + 8, MINE), F32)],
        **whole([((32, PART, MINE), BF)]),
        name="expert",
    )(rows, down, gate, up, own_g, own_u, w_from_prev, w_from_next)
    returned = lax.all_to_all(terms, "exp", 0, 0, tiled=True)
    (sums,) = pl.pallas_call(
        combine_kernel,
        in_specs=[VMEM] * 2,
        out_specs=[VMEM],
        **whole([((BLOCKS, PART, TOK), BF)]),
        name="combine",
    )(returned, places)
    bands = lax.all_to_all(sums, "zh", 0, 0, tiled=True)

    pad = ((0, PART - COLS), (0, 0))
    router_cols = jnp.pad(lax.dynamic_slice_in_dim(router_weight, first, COLS, 0), pad)
    gain = jnp.pad(lax.dynamic_slice_in_dim(norm_gain, first, COLS, 0)[:, None], pad)
    values = jnp.pad(values, pad)
    (attended,) = pl.pallas_call(
        project_kernel,
        in_specs=[VMEM] * 7,
        out_specs=[VMEM],
        **whole([((PART, TOK), F32)]),
        name="project",
    )(all_grads, rows, jnp.pad(key_weight, pad), jnp.pad(value_weight, pad), router_cols, shares, routes_t)
    lifted, stat = pl.pallas_call(
        lift_kernel,
        in_specs=[VMEM] * 4,
        out_specs=[VMEM] * 2,
        **whole([((PART, TOK), F32), ((32, TOK), F32)]),
        name="lift",
    )(bands, attended, gain, values)
    stats = lax.all_to_all(stat, "exp", 0, 0, tiled=True)
    (result,) = pl.pallas_call(
        finish_kernel,
        in_specs=[VMEM] * 5,
        out_specs=[VMEM],
        **whole([((COLS, TOK), F32)]),
        name="finish",
    )(stats, lifted, values, inverse, seed_grad.T + adjoint_cols)
    return result.T


def solution(mesh):
    finer = Mesh(mesh.devices.reshape(8, 2, 32), ("zh", "zl", "exp"))
    placed = (
        P(SEQ, None),
        P(SEQ, "exp"),
        P(SEQ, None),
        P(),
        P(),
        P(SEQ, None),
        P(SEQ, None, "exp"),
        P(SEQ, "exp"),
        P(SEQ, None),
        P(SEQ, None),
        P(None, "exp"),
        P("exp", None),
        P("exp", None),
        P("exp", None),
        P("exp", None, SEQ),
        P("exp", None, SEQ),
        P("exp", SEQ, None),
        P("exp", None, SEQ),
        P("exp", None, SEQ),
    )
    return jax.shard_map(
        on_device, mesh=finer, in_specs=placed, out_specs=P(SEQ, "exp"), check_vma=False
    )
```

time: 391 us -> 197 us (0.50)
  waiting for transfers between devices: 334 us -> 49 us
  starting transfers between devices: 12.3 us -> 52 us
  blocking collectives: 0 us -> 34.2 us
  Pallas kernels: 0 us -> 22.6 us
  local copies, waits for them, and re-layouts: 3.87 us -> 20.7 us
  matrix products: 15.5 us -> 0 us
  other arithmetic: 10.6 us -> 3.39 us
    psum x1 -> x0, waiting for transfers between devices: 137 us -> none  [on_device(): lax.psum(kv_back.astype(jnp.bfloat16), 'exp').astype(jnp.float32)]
    ppermute x2 -> x4, waiting for transfers between devices: 124 us -> 19.1 us  [the longest x1 18 us: on_device(): w_from_prev = lax.ppermute(w_next, SEQ, to_next)]
    all_gather x1, waiting for transfers between devices: 72.6 us -> 0.02 us  [on_device(): all_grads = lax.all_gather(grads, 'exp', axis=0)]
    all_to_all x0 -> x1, blocking collectives: none -> 34.2 us  [on_device(): returned = lax.all_to_all(terms, 'exp', 0, 0, tiled=True)]
    all_to_all x1 -> x4, starting transfers between devices: 6.98 us -> 40.2 us  [the longest x1 15.6 us: on_device(): lax.all_to_all(jnp.broadcast_to(pay[None], (BLOCKS, PART + 16, TOK)), 'zh...]
    all_to_all x1 -> x4, waiting for transfers between devices: 0.01 us -> 29.9 us  [the longest x1 12.8 us: on_device(): lax.all_to_all(jnp.broadcast_to(pay[None], (BLOCKS, PART + 16, TOK)), 'zh...]
    pallas_call x0 -> x9, Pallas kernels: none -> 22.6 us  [the longest x1 7.7 us: on_device(): pl.pallas_call(dispatch_kernel, in_specs=[VMEM] * 2, out_specs=[VMEM] * 3...]
    dot_general x14 -> x0, matrix products: 15.5 us -> none  [the longest x1 2.99 us: on_device(): jnp.einsum('nd,fd->nf', lax.all_gather(expert_input, 'seq', axis=0, tiled...]
  transfers between devices with their start and end apart: 5 -> 9, of which waited for: 3 -> 5; matrix products, arithmetic and copies ran while one was open for 1% -> 3% of each run, Pallas kernels for 0% -> 6%
where the time goes in v1:
time: 197 us; the launch traced here: 196 us
  starting transfers between devices  52 us (26%)
  waiting for transfers between devices  49 us (25%)
  blocking collectives  34.2 us (17%)
  Pallas kernels  22.6 us (11%)
  local copies, waits for them, and re-layouts  20.7 us (11%)
  between operations  13.7 us (7%)
  other arithmetic  3.39 us (2%)
    all_to_all x1, blocking collectives, on_device(): returned = lax.all_to_all(terms, 'exp', 0, 0, tiled=True)  34.2 us
    ppermute x1, waiting for transfers between devices, on_device(): w_from_prev = lax.ppermute(w_next, SEQ, to_next)  18 us
    unnamed x57, local copies, waits for them, and re-layouts  15.8 us
    all_to_all x1, starting transfers between devices, on_device(): lax.all_to_all(jnp.broadcast_to(pay[None], (BLOCKS, PART + 16, TOK)), 'zh...  15.6 us
    all_to_all x1, waiting for transfers between devices, on_device(): lax.all_to_all(jnp.broadcast_to(pay[None], (BLOCKS, PART + 16, TOK)), 'zh...  12.8 us
    all_to_all x1, starting transfers between devices, on_device(): rows = lax.all_to_all(sent, 'exp', 0, 0, tiled=True)  12.4 us
    all_to_all x1, waiting for transfers between devices, on_device(): bands = lax.all_to_all(sums, 'zh', 0, 0, tiled=True)  11 us
    pallas_call x1, Pallas kernels, on_device(): pl.pallas_call(dispatch_kernel, in_specs=[VMEM] * 2, out_specs=[VMEM] * 3...  7.7 us
  transfers between devices with their start and end apart: 9, of which 5 were waited for; matrix products, arithmetic and copies ran while one was open for 3% of the time, Pallas kernels for 6%

profile of v1, /device:TPU:1, one launch (start us, length us, event | category | flops | bytes accessed | tf_op | source)
XLA Modules:
  0.0 195.5 jit_solution(9613560517602445397)
XLA Ops:
  7.5 1.1 copy-done.10
  8.6 1.1 copy-done.11
  9.7 1.0 copy-done.12
  12.3 1.3 route.1
  14.3 15.6 %all-to-all-start = ((bf16[8,112,128]{2,1,0:T(8,128)(2,1)}), bf16[8,112,128]{2,1,0:T(8,128)(2,1)S(1)}, u32[]{:S(2)}, u32[]{:S(2)}) async-start(bf16[8,112,128]{2,1,0:T(8,128)(2,1)} %broadcast_in_dim.14), calls=%async_computation | async-start | bytes 458752 | tf_op jit(solution)/shard_map/all_to_all | solution.py:335
  30.0 1.1 pack.1
  32.0 1.0 copy-done.23
  33.0 12.8 %all-to-all-done.gathered = bf16[8,112,128]{2,1,0:T(8,128)(2,1)S(1)} async-done(((bf16[8,112,128]{2,1,0:T(8,128)(2,1)}), bf16[8,112,128]{2,1,0:T(8,128)(2,1)S(1)}, u32[]{:S(2)}, u32[]{:S(2)}) %all-to-all-start) | async-done | bytes 229408 | tf_op jit(solution)/shard_map/all_to_all | solution.py:335
  45.8 7.7 %dispatch.1 = (bf16[32,128,256]{2,1,0:T(8,128)(2,1)S(1)}, f32[32,1024]{1,0:T(8,128)S(1)}, f32[32,1024]{1,0:T(8,128)}) custom-call(bf16[8,112,128]{2,1,0:T(8,128)(2,1)S(1)} %all-to-all-done.gathered, bf16[32,32,256]{2,1,0:T(8,128)(2,1)S(1)} %get-tuple-element.19.query_parts), custom_call_target="tpu_custom_call" | custom-call | tf_op jit(solution)/shard_map/dispatch/pallas_call | solution.py:371
  53.5 1.3 copy-done.4
  54.9 12.4 %all-to-all-start.1 = ((bf16[32,128,256]{2,1,0:T(8,128)(2,1)}), bf16[32,128,256]{2,1,0:T(8,128)(2,1)S(1)}, u32[]{:S(2)}, u32[]{:S(2)}) async-start(bf16[32,128,256]{2,1,0:T(8,128)(2,1)} %copy-done.4), calls=%async_computation.1 | async-start | bytes 4194304 | tf_op jit(solution)/shard_map/all_to_all | solution.py:378
  68.9 1.9 collective-permute-start.3
  70.9 3.4 %collective-permute-start.2 = (bf16[128,128]{1,0:T(8,128)(2,1)S(1)}, bf16[128,128]{1,0:T(8,128)(2,1)}, u32[]{:S(2)}, u32[]{:S(2)}) collective-permute-start(bf16[128,128]{1,0:T(8,128)(2,1)S(1)} %pad_maximum_fusion.kv), channel_id=1, source_target_pairs={{0,32},{32,64},{64,96},{96,128},{128,160},{160,192},{192,224},{224... | collective-permute-start | bytes 98312 | tf_op jit(solution)/shard_map/ppermute | solution.py:344
  75.0 1.0 fusion.aligned
  76.0 1.0 collective-permute-done.2.kv_prev
  77.0 1.9 attend.1
  78.9 2.2 %collective-permute-start = (bf16[160,2880]{1,0:T(8,128)(2,1)}, bf16[160,2880]{1,0:T(8,128)(2,1)S(1)}, u32[]{:S(2)}, u32[]{:S(2)}) collective-permute-start(bf16[160,2880]{1,0:T(8,128)(2,1)} %copy-done.23), channel_id=1, source_target_pairs={{0,32},{32,64},{64,96},{96,128},{128,160},{160,192},{192,224},{224... | collective-permute-start | bytes 2764808 | tf_op jit(solution)/shard_map/ppermute | solution.py:356
  81.1 4.3 %collective-permute-start.1 = (bf16[160,2880]{1,0:T(8,128)(2,1)}, bf16[160,2880]{1,0:T(8,128)(2,1)S(1)}, u32[]{:S(2)}, u32[]{:S(2)}) collective-permute-start(bf16[160,2880]{1,0:T(8,128)(2,1)} %copy-done.22), channel_id=1, source_target_pairs={{32,0},{64,32},{96,64},{128,96},{160,128},{192,160},{224,192},{256... | collective-permute-start | bytes 2764808 | tf_op jit(solution)/shard_map/ppermute | solution.py:357
  85.4 18.0 %collective-permute-done.from_prev = bf16[160,2880]{1,0:T(8,128)(2,1)S(1)} collective-permute-done((bf16[160,2880]{1,0:T(8,128)(2,1)}, bf16[160,2880]{1,0:T(8,128)(2,1)S(1)}, u32[]{:S(2)}, u32[]{:S(2)}) %collective-permute-start) | collective-permute-done | bytes 921632 | tf_op jit(solution)/shard_map/ppermute | solution.py:356
  103.4 1.0 copy-done.6
  104.4 0.9 copy-done.8
  105.4 1.1 copy-done.3
  106.4 1.2 copy-done.7
  107.6 1.2 copy-done.9
  109.6 1.8 expert.1
  111.4 34.2 %all_to_all.31.returned = bf16[32,96,256]{2,1,0:T(8,128)(2,1)S(1)} all-to-all(bf16[32,96,256]{2,1,0:T(8,128)(2,1)S(1)} %expert.1), channel_id=1, replica_groups=mesh['zh'=8,'zl'=2,'exp'=32] {'exp'}, dimensions={0} | all-to-all | bytes 3145728 | tf_op jit(solution)/shard_map/all_to_all | solution.py:387
  145.6 6.8 %combine.1 = bf16[8,96,128]{2,1,0:T(8,128)(2,1)} custom-call(bf16[32,96,256]{2,1,0:T(8,128)(2,1)S(1)} %all_to_all.31.returned, f32[32,1024]{1,0:T(8,128)S(1)} %get-tuple-element.25.places), custom_call_target="tpu_custom_call" | custom-call | tf_op jit(solution)/shard_map/combine/pallas_call | solution.py:388
  152.4 5.4 %all-to-all-start.3 = ((bf16[8,96,128]{2,1,0:T(8,128)(2,1)}), bf16[8,96,128]{2,1,0:T(8,128)(2,1)S(1)}, u32[]{:S(2)}, u32[]{:S(2)}) async-start(bf16[8,96,128]{2,1,0:T(8,128)(2,1)} %combine.1), calls=%async_computation.3 | async-start | bytes 393216 | tf_op jit(solution)/shard_map/all_to_all | solution.py:395
  160.4 1.4 copy-done.5
  162.6 11.0 %all-to-all-done.3.bands = bf16[8,96,128]{2,1,0:T(8,128)(2,1)S(1)} async-done(((bf16[8,96,128]{2,1,0:T(8,128)(2,1)}), bf16[8,96,128]{2,1,0:T(8,128)(2,1)S(1)}, u32[]{:S(2)}, u32[]{:S(2)}) %all-to-all-start.3) | async-done | bytes 196640 | tf_op jit(solution)/shard_map/all_to_all | solution.py:395
  174.3 6.9 %all-to-all-start.4 = ((f32[32,1,128]{2,1,0:T(1,128)}), f32[32,1,128]{2,1,0:T(1,128)S(1)}, u32[]{:S(2)}, u32[]{:S(2)}) async-start(f32[32,1,128]{2,1,0:T(1,128)} %bitcast.24), calls=%async_computation.4 | async-start | bytes 32768 | tf_op jit(solution)/shard_map/all_to_all | solution.py:415
  182.0 6.1 %all-to-all-done.4 = f32[32,1,128]{2,1,0:T(1,128)S(1)} async-done(((f32[32,1,128]{2,1,0:T(1,128)}), f32[32,1,128]{2,1,0:T(1,128)S(1)}, u32[]{:S(2)}, u32[]{:S(2)}) %all-to-all-start.4) | async-done | bytes 16416 | tf_op jit(solution)/shard_map/all_to_all | solution.py:415
  (72 shorter events, 13.0 us)
Async XLA Ops:
  6.5 23.4 %copy-start.2 = (bf16[1,2880,96]{1,2,0:T(8,128)(2,1)S(1)}, bf16[1,2880,96]{1,2,0:T(8,128)(2,1)}, u32[]{:S(2)}) copy-start(bf16[1,2880,96]{1,2,0:T(8,128)(2,1)} %param.34) | copy-start | bytes 1658884
  6.5 23.4 %copy-start = (bf16[1,96,2880]{2,1,0:T(8,128)(2,1)S(1)}, bf16[1,96,2880]{2,1,0:T(8,128)(2,1)}, u32[]{:S(2)}) copy-start(bf16[1,96,2880]{2,1,0:T(8,128)(2,1)} %param.35) | copy-start | bytes 1658884
  6.5 23.4 %copy-start.1 = (bf16[1,2880,96]{1,2,0:T(8,128)(2,1)S(1)}, bf16[1,2880,96]{1,2,0:T(8,128)(2,1)}, u32[]{:S(2)}) copy-start(bf16[1,2880,96]{1,2,0:T(8,128)(2,1)} %param.33) | copy-start | bytes 1658884
  7.5 1.1 copy-start.10
  8.6 1.1 copy-start.11
  9.7 1.0 copy-start.12
  12.3 17.7 %copy-start.13 = (bf16[2880,64]{0,1:T(8,128)(2,1)S(1)}, bf16[2880,64]{0,1:T(8,128)(2,1)}, u32[]{:S(2)}) copy-start(bf16[2880,64]{0,1:T(8,128)(2,1)} %param.29) | copy-start | bytes 1105924
  12.3 17.7 %copy-start.15 = (bf16[1,512,96]{1,2,0:T(8,128)(2,1)S(1)}, bf16[1,512,96]{1,2,0:T(8,128)(2,1)}, u32[]{:S(2)}) copy-start(bf16[1,512,96]{1,2,0:T(8,128)(2,1)} %param.36) | copy-start | bytes 294916
  12.3 17.7 %copy-start.16 = (bf16[1,512,96]{1,2,0:T(8,128)(2,1)S(1)}, bf16[1,512,96]{1,2,0:T(8,128)(2,1)}, u32[]{:S(2)}) copy-start(bf16[1,512,96]{1,2,0:T(8,128)(2,1)} %param.37) | copy-start | bytes 294916
  14.3 31.5 %all-to-all-start = ((bf16[8,112,128]{2,1,0:T(8,128)(2,1)}), bf16[8,112,128]{2,1,0:T(8,128)(2,1)S(1)}, u32[]{:S(2)}, u32[]{:S(2)}) async-start(bf16[8,112,128]{2,1,0:T(8,128)(2,1)} %broadcast_in_dim.14), calls=%async_computation | async-start | bytes 458752 | tf_op jit(solution)/shard_map/all_to_all | solution.py:335
  32.0 1.0 copy-start.23
  33.0 21.9 %copy-start.18 = (bf16[96,256]{1,0:T(8,128)(2,1)}, bf16[96,256]{1,0:T(8,128)(2,1)S(1)}, u32[]{:S(2)}) copy-start(bf16[96,256]{1,0:T(8,128)(2,1)S(1)} %get-tuple-element.22.own_u) | copy-start | bytes 147460
  53.5 1.4 copy-start.4
  54.9 12.4 %copy-start.27 = (bf16[128,256]{1,0:T(8,128)(2,1)S(1)}, bf16[128,256]{1,0:T(8,128)(2,1)}, u32[]{:S(2)}) copy-start(bf16[128,256]{1,0:T(8,128)(2,1)} %param.28) | copy-start | bytes 196612
  54.9 13.3 %copy-start.17 = (bf16[128,64]{0,1:T(8,128)(2,1)S(1)}, bf16[128,64]{0,1:T(8,128)(2,1)}, u32[]{:S(2)}) copy-start(bf16[128,64]{0,1:T(8,128)(2,1)} %param.26) | copy-start | bytes 49156
  54.9 50.5 %all-to-all-start.1 = ((bf16[32,128,256]{2,1,0:T(8,128)(2,1)}), bf16[32,128,256]{2,1,0:T(8,128)(2,1)S(1)}, u32[]{:S(2)}, u32[]{:S(2)}) async-start(bf16[32,128,256]{2,1,0:T(8,128)(2,1)} %copy-done.4), calls=%async_computation.1 | async-start | bytes 4194304 | tf_op jit(solution)/shard_map/all_to_all | solution.py:378
  67.2 93.2 %all-gather.3.cloned.1.call-start = ((), (), s32[]{:S(2)}) async-start(), calls=%async_computation.5 | async-start | bytes 1757184 | tf_op jit(solution)/shard_map/all_gather | solution.py:369
  68.9 8.2 %collective-permute-start.3 = (bf16[256,128]{1,0:T(8,128)(2,1)}, bf16[256,128]{1,0:T(8,128)(2,1)S(1)}, u32[]{:S(2)}, u32[]{:S(2)}) collective-permute-start(bf16[256,128]{1,0:T(8,128)(2,1)} %maximum_maximum_fusion), channel_id=1, source_target_pairs={{32,0},{64,32},{96,64},{128,96},{160,128},{192,160},{224,192},{256... | collective-permute-start | bytes 196616 | tf_op jit(solution)/shard_map/ppermute | solution.py:345
  70.9 6.2 %collective-permute-start.2 = (bf16[128,128]{1,0:T(8,128)(2,1)S(1)}, bf16[128,128]{1,0:T(8,128)(2,1)}, u32[]{:S(2)}, u32[]{:S(2)}) collective-permute-start(bf16[128,128]{1,0:T(8,128)(2,1)S(1)} %pad_maximum_fusion.kv), channel_id=1, source_target_pairs={{0,32},{32,64},{64,96},{96,128},{128,160},{160,192},{192,224},{224... | collective-permute-start | bytes 98312 | tf_op jit(solution)/shard_map/ppermute | solution.py:344
  78.9 24.5 %collective-permute-start = (bf16[160,2880]{1,0:T(8,128)(2,1)}, bf16[160,2880]{1,0:T(8,128)(2,1)S(1)}, u32[]{:S(2)}, u32[]{:S(2)}) collective-permute-start(bf16[160,2880]{1,0:T(8,128)(2,1)} %copy-done.23), channel_id=1, source_target_pairs={{0,32},{32,64},{64,96},{96,128},{128,160},{160,192},{192,224},{224... | collective-permute-start | bytes 2764808 | tf_op jit(solution)/shard_map/ppermute | solution.py:356
  81.1 23.3 %collective-permute-start.1 = (bf16[160,2880]{1,0:T(8,128)(2,1)}, bf16[160,2880]{1,0:T(8,128)(2,1)S(1)}, u32[]{:S(2)}, u32[]{:S(2)}) collective-permute-start(bf16[160,2880]{1,0:T(8,128)(2,1)} %copy-done.22), channel_id=1, source_target_pairs={{32,0},{64,32},{96,64},{128,96},{160,128},{192,160},{224,192},{256... | collective-permute-start | bytes 2764808 | tf_op jit(solution)/shard_map/ppermute | solution.py:357
  103.4 1.0 copy-start.6
  105.4 1.1 copy-start.3
  106.4 1.2 copy-start.7
  107.6 1.2 copy-start.9
  145.6 13.1 %copy-start.24 = (bf16[90,256]{1,0:T(8,128)(2,1)S(1)}, bf16[90,256]{1,0:T(8,128)(2,1)}, u32[]{:S(2)}) copy-start(bf16[90,256]{1,0:T(8,128)(2,1)} %param.30) | copy-start | bytes 138244
  145.6 13.1 %copy-start.25 = (bf16[90,256]{1,0:T(8,128)(2,1)S(1)}, bf16[90,256]{1,0:T(8,128)(2,1)}, u32[]{:S(2)}) copy-start(bf16[90,256]{1,0:T(8,128)(2,1)} %param.31) | copy-start | bytes 138244
  145.6 14.8 %copy-start.21 = (s32[128,4]{0,1:T(4,128)S(1)}, s32[128,4]{0,1:T(4,128)}, u32[]{:S(2)}) copy-start(s32[128,4]{0,1:T(4,128)} %param.24) | copy-start | bytes 6148
  152.4 21.3 %all-to-all-start.3 = ((bf16[8,96,128]{2,1,0:T(8,128)(2,1)}), bf16[8,96,128]{2,1,0:T(8,128)(2,1)S(1)}, u32[]{:S(2)}, u32[]{:S(2)}) async-start(bf16[8,96,128]{2,1,0:T(8,128)(2,1)} %combine.1), calls=%async_computation.3 | async-start | bytes 393216 | tf_op jit(solution)/shard_map/all_to_all | solution.py:395
  160.4 1.5 copy-start.5
  161.9 19.3 %copy-start.26 = (f32[128,90]{0,1:T(8,128)S(1)}, f32[128,90]{0,1:T(8,128)}, u32[]{:S(2)}) copy-start(f32[128,90]{0,1:T(8,128)} %param.20) | copy-start | bytes 138244
  174.3 13.7 %all-to-all-start.4 = ((f32[32,1,128]{2,1,0:T(1,128)}), f32[32,1,128]{2,1,0:T(1,128)S(1)}, u32[]{:S(2)}, u32[]{:S(2)}) async-start(f32[32,1,128]{2,1,0:T(1,128)} %bitcast.24), calls=%async_computation.4 | async-start | bytes 32768 | tf_op jit(solution)/shard_map/all_to_all | solution.py:415
  (5 other events, 4.3 us)
Sparse Core Ops, SparseCore 0:
  79.0 61.5 all-gather.2

commit v2 on v1

--- a/solution.py
+++ b/solution.py
@@ -19,7 +19,7 @@
 HALF = BAND // 2
 COLS = D // 32
 PART = 96
-SENDERS = D // PART
+WIDE = D + TOK // 2
 BLOCKS = 8
 MINE = BLOCKS * CAP
 EPSILON = 1e-05
@@ -47,23 +47,28 @@
     return high, (value - high.astype(F32)).astype(BF)
 
 
-def whole(shape_dtypes, flops=0, moved=0):
-    return dict(
-        out_shape=[jax.ShapeDtypeStruct(s, d) for s, d in shape_dtypes],
-        compiler_params=pltpu.CompilerParams(vmem_limit_bytes=40 * 1024 * 1024),
-        cost_estimate=pl.CostEstimate(flops=flops, bytes_accessed=moved, transcendentals=0),
-    )
-
-
-SMEM = pl.BlockSpec(memory_space=pltpu.SMEM)
-VMEM = pl.BlockSpec(memory_space=pltpu.VMEM)
+def run(kernel, name, args, outs, scratch=(), room=16):
+    def spec(shape):
+        return pl.BlockSpec(shape, lambda i: (0,) * len(shape))
+
+    scalars = pl.BlockSpec(memory_space=pltpu.SMEM)
+    return pl.pallas_call(
+        kernel,
+        grid=(1,),
+        in_specs=[scalars if a.dtype == jnp.int32 and a.ndim == 1 else spec(a.shape) for a in args],
+        out_specs=[spec(shape) for shape, _ in outs],
+        out_shape=[jax.ShapeDtypeStruct(shape, dtype) for shape, dtype in outs],
+        scratch_shapes=list(scratch),
+        compiler_params=pltpu.CompilerParams(vmem_limit_bytes=room * 1024 * 1024),
+        name=name,
+    )(*args)
 
 
 def route_kernel(where, layer, gain, router, routes, adjoint, out_w, pay, inverse, shares, out_back):
     values = layer[...].astype(F32)
     inv = lax.rsqrt(jnp.sum(values * values, axis=0, keepdims=True) / D + EPSILON)
     inverse[...] = inv
-    high, low = split(router[...].astype(F32) * gain[...])
+    high, low = split(router[...].astype(F32) * gain[...].reshape(1, D))
     logits = (dot(high, layer[...]) + dot(low, layer[...])) * inv
     names = rows_of((EXPERTS, TOK))
     picked = [names == routes[k : k + 1, :] for k in range(TOPK)]
@@ -74,22 +79,49 @@
     taken = sum(p.astype(F32) for p in picked)
     earlier = (rows_of((TOK, TOK)) < lanes_of((TOK, TOK))).astype(BF)
     ranks = dot(taken.astype(BF), earlier)
-    line = rows_of((16, TOK))
-    meta = jnp.zeros((16, TOK), F32)
+    line = rows_of((2 * TOPK, TOK))
+    meta = jnp.zeros((2 * TOPK, TOK), F32)
+    place = jnp.full((1, TOK), -1.0, F32)
+    gate = jnp.zeros((1, TOK), F32)
     for k in range(TOPK):
         share = raised[k] / total
         shares[k : k + 1, :] = share
         rank = jnp.sum(jnp.where(picked[k], ranks, 0.0), axis=0, keepdims=True)
-        meta = jnp.where(line == k, routes[k : k + 1, :].astype(F32), meta)
+        name = routes[k : k + 1, :]
+        meta = jnp.where(line == k, name.astype(F32), meta)
         meta = jnp.where(line == TOPK + k, rank, meta)
-        meta = jnp.where(line == 2 * TOPK + k, share, meta)
-    start = pl.multiple_of(jnp.minimum(where[0], SENDERS - 1) * PART, PART)
-    pay[0:PART, :] = adjoint[pl.ds(start, PART), :]
-    pay[PART:, :] = meta.astype(BF)
+        place = jnp.where(name == where[0], rank, place)
+        gate = jnp.where(name == where[0], share, gate)
+    placing = jnp.where(rows_of((CAP, TOK)).astype(F32) == place, gate, 0.0).astype(BF)
+    pay[:, 0:D] = dot(placing, adjoint[...], ((1,), (1,))).astype(BF)
+    tail = jnp.concatenate(
+        [meta[:, : TOK // 2], meta[:, TOK // 2 :], jnp.zeros((16, TOK // 2), F32)], axis=0
+    )
+    pay[:, D:] = tail.astype(BF)
     out_back[...] = dot(out_w[...], adjoint[...]).astype(BF)
 
 
-def pack_kernel(where, down, gate, up, store_g, store_u, query_w, to_next, to_prev, own_g, own_u, query_parts):
+def slots_kernel(metas, places):
+    names = rows_of((EXPERTS, TOK)).astype(F32)
+    for b in range(BLOCKS):
+        tail = metas[b, :, :].astype(F32)
+        meta = jnp.concatenate([tail[0 : 2 * TOPK, :], tail[2 * TOPK :, :]], axis=1)
+        place = jnp.full((EXPERTS, TOK), -1.0, F32)
+        for k in range(TOPK):
+            match = names == meta[k : k + 1, :]
+            place = jnp.where(match, meta[TOPK + k : TOPK + k + 1, :], place)
+        places[:, b * TOK : (b + 1) * TOK] = place
+
+
+def share_kernel(query_w, parts):
+    for c in range(32):
+        piece = query_w[:, c * COLS : (c + 1) * COLS]
+        parts[c, :, :] = jnp.zeros((32, 256), BF)
+        parts[c, :, 0:COLS] = piece[0:32]
+        parts[c, :, 128 : 128 + COLS] = piece[32:64]
+
+
+def pack_kernel(where, down, gate, up, store_g, store_u, to_next, to_prev, own_g, own_u):
     def chosen(parity):
         i, j = rows_of((16 * CAP, MINE)), lanes_of((16 * CAP, MINE))
         return (i == (2 * (j // CAP) + parity) * CAP + j % CAP).astype(BF)
@@ -108,11 +140,6 @@
             for m in range(3):
                 lane = (3 * n + m) * MINE
                 ref[3 * HALF :, lane : lane + MINE] = sent[first + 16 * m : first + 16 * m + 16, :]
-    for c in range(32):
-        piece = query_w[:, c * COLS : (c + 1) * COLS]
-        query_parts[c, :, :] = jnp.zeros((32, 256), BF)
-        query_parts[c, :, 0:COLS] = piece[0:32]
-        query_parts[c, :, 128 : 128 + COLS] = piece[32:64]
 
 
 def attend_kernel(where, query, out_back, kv, kv_prev, next_q, aligned, grads):
@@ -164,41 +191,9 @@
     grads[192:208, :] = tail.astype(BF)
 
 
-def dispatch_kernel(gathered, query_parts, sent, places, gates):
-    names = rows_of((EXPERTS, TOK)).astype(F32)
-    for b in range(BLOCKS):
-        meta = gathered[b, PART:, :].astype(F32)
-        place = jnp.full((EXPERTS, TOK), -1.0, F32)
-        gate = jnp.zeros((EXPERTS, TOK), F32)
-        for k in range(TOPK):
-            match = names == meta[k : k + 1, :]
-            place = jnp.where(match, meta[TOPK + k : TOPK + k + 1, :] + CAP * (b % 4), place)
-            gate = jnp.where(match, meta[2 * TOPK + k : 2 * TOPK + k + 1, :], gate)
-        places[:, b * TOK : (b + 1) * TOK] = place
-        gates[:, b * TOK : (b + 1) * TOK] = gate
-    features = [
-        jnp.concatenate([gathered[b, 0:PART, :] for b in range(4 * h, 4 * h + 4)], axis=1)
-        for h in range(2)
-    ]
-    slot = rows_of((TOK, 4 * TOK)).astype(F32)
-
-    def step(e, carry):
-        for h in range(2):
-            lanes = slice(h * 4 * TOK, (h + 1) * 4 * TOK)
-            placing = jnp.where(
-                slot == places[pl.ds(e, 1), lanes], gates[pl.ds(e, 1), lanes], 0.0
-            ).astype(BF)
-            sent[e, 0:PART, h * TOK : (h + 1) * TOK] = dot(
-                features[h], placing, ((1,), (1,))
-            ).astype(BF)
-        return carry
-
-    lax.fori_loop(0, EXPERTS, step, 0)
-    sent[:, PART:, :] = query_parts[...]
-
-
 def expert_kernel(rows, down, gate, up, own_g, own_u, from_prev, from_next, sent, total):
-    features = rows[0:SENDERS, 0:PART, :].reshape(D, MINE)
+    features = rows[:, :, 0:D].reshape(MINE, D)
+    across = ((1,), (1,))
 
     def act(hidden, g, u):
         g, u = g.astype(F32), u.astype(F32)
@@ -213,9 +208,9 @@
             [ref[3 * HALF :, (3 * n + m) * MINE : (3 * n + m + 1) * MINE] for m in range(3)], axis=0
         )
 
-    backs = list(act(dot(down[...], features), own_g[...], own_u[...]))
+    backs = list(act(dot(down[...], features, across), own_g[...], own_u[...]))
     for ref in (from_prev, from_next):
-        backs += list(act(dot(ref[0:HALF, :], features), stored(ref, 0), stored(ref, 1)))
+        backs += list(act(dot(ref[0:HALF, :], features, across), stored(ref, 0), stored(ref, 1)))
     weights = [gate[...], up[...]]
     for ref in (from_prev, from_next):
         weights += [ref[HALF : 2 * HALF, :], ref[2 * HALF : 3 * HALF, :]]
@@ -228,20 +223,19 @@
 
 
 def combine_kernel(returned, places, sent):
-    slot = rows_of((TOK, 4 * TOK)).astype(F32)
-
+    slot = rows_of((CAP, TOK)).astype(F32)
+    empty = jnp.zeros((CAP, TOK), BF)
     for h in range(2):
-        lanes = slice(h * 4 * TOK, (h + 1) * 4 * TOK)
-
-        def step(i, total):
-            picks, terms = [], []
-            for n in range(2):
-                e = 2 * i + n
-                picks.append((slot == places[pl.ds(e, 1), lanes]).astype(BF))
-                terms.append(returned[e, :, h * TOK : (h + 1) * TOK])
-            return total + dot(jnp.concatenate(terms, axis=1), jnp.concatenate(picks, axis=0))
-
-        total = lax.fori_loop(0, EXPERTS // 2, step, jnp.zeros((PART, 4 * TOK), F32))
+        total = jnp.zeros((PART, 4 * TOK), F32)
+        for pair in range(0, EXPERTS, 2):
+            picks = []
+            for e in (pair, pair + 1):
+                for b in range(4):
+                    lanes = slice((4 * h + b) * TOK, (4 * h + b + 1) * TOK)
+                    pick = (slot == places[e : e + 1, lanes]).astype(BF)
+                    picks.append(jnp.concatenate([empty] * b + [pick] + [empty] * (3 - b), axis=1))
+            terms = [returned[e, :, h * TOK : (h + 1) * TOK] for e in (pair, pair + 1)]
+            total = total + dot(jnp.concatenate(terms, axis=1), jnp.concatenate(picks, axis=0))
         for b in range(4):
             sent[4 * h + b, :, :] = total[:, b * TOK : (b + 1) * TOK].astype(BF)
 
@@ -250,7 +244,7 @@
     total = jnp.zeros((PART, TOK), F32)
     for h in range(QH):
         for n in range(2):
-            weight = rows[h, PART:, n * 128 : n * 128 + PART]
+            weight = rows[h, :, n * 128 : n * 128 + PART]
             total = total + dot(weight, grads[h, 32 * n : 32 * n + 32, :], ((0,), (0,)))
     group = QH // KVH
     for first, weight in ((64, key_w), (128, value_w)):
@@ -321,21 +315,34 @@
     parity = lax.axis_index("zl")
     where = jnp.stack([col, parity, block]).astype(jnp.int32)
     first = col * COLS
-    adjoint_t, layer_t, routes_t = adjoint.T, layer_input.T, routes.T
+    adjoint_t, layer_t, routes_t, router_t = adjoint.T, layer_input.T, routes.T, router_weight.T
     to_next = [(i, (i + 1) % 16) for i in range(16)]
     to_prev = [(j, i) for i, j in to_next]
 
-    pay, inverse, shares, out_back = pl.pallas_call(
+    pay, inverse, shares, out_back = run(
         route_kernel,
-        in_specs=[SMEM] + [VMEM] * 6,
-        out_specs=[VMEM] * 4,
-        **whole([((PART + 16, TOK), BF), ((1, TOK), F32), ((TOPK, TOK), F32), ((HEAD_DIM, TOK), BF)]),
-        name="route",
-    )(where, layer_t, norm_gain[None, :], router_weight.T, routes_t, adjoint_t, output_weight)
-    gathered = lax.all_to_all(
-        jnp.broadcast_to(pay[None], (BLOCKS, PART + 16, TOK)), "zh", 0, 0, tiled=True
-    )
-
+        "route",
+        (where, layer_t, norm_gain, router_t, routes_t, adjoint_t, output_weight),
+        [((CAP, WIDE), BF), ((1, TOK), F32), ((TOPK, TOK), F32), ((HEAD_DIM, TOK), BF)],
+        room=60,
+    )
+    gathered = lax.all_gather(pay, "zh", axis=0)
+
+    down, gate, up = down_weight[0], gate_weight[0].T, up_weight[0].T
+    wide, narrow = ((3 * HALF + 16, D), BF), ((BAND, MINE), BF)
+    w_next, w_prev, own_g, own_u = run(
+        pack_kernel,
+        "pack",
+        (where, down, gate, up, stored_gate[0].T, stored_up[0].T),
+        [wide, wide, narrow, narrow],
+    )
+
+    w_next, w_prev, query_weight = lax.optimization_barrier((w_next, w_prev, query_weight))
+    w_from_prev = lax.ppermute(w_next, SEQ, to_next)
+    w_from_next = lax.ppermute(w_prev, SEQ, to_prev)
+
+    (query_parts,) = run(share_kernel, "share", (query_weight.T,), [((32, 32, 256), BF)])
+    query_cols = lax.all_to_all(query_parts, "exp", 0, 0, tiled=True)
     kv_start = col // (QH // KVH) * HEAD_DIM
     kv = jnp.concatenate(
         [lax.dynamic_slice_in_dim(a, kv_start, HEAD_DIM, 1) for a in (stored_key, stored_value)], axis=1
@@ -343,83 +350,55 @@
     query_t = stored_query.T
     kv_prev = lax.ppermute(kv, SEQ, to_next)
     from_next_q = lax.ppermute(jnp.concatenate([query_t, out_back, kv], axis=0), SEQ, to_prev)
-
-    down, gate, up = down_weight[0], gate_weight[0].T, up_weight[0].T
-    wide, narrow = ((3 * HALF + 16, D), BF), ((BAND, MINE), BF)
-    w_next, w_prev, own_g, own_u, query_parts = pl.pallas_call(
-        pack_kernel,
-        in_specs=[SMEM] + [VMEM] * 6,
-        out_specs=[VMEM] * 5,
-        **whole([wide, wide, narrow, narrow, ((32, 32, 256), BF)]),
-        name="pack",
-    )(where, down, gate, up, stored_gate[0].T, stored_up[0].T, query_weight.T)
-    w_from_prev = lax.ppermute(w_next, SEQ, to_next)
-    w_from_next = lax.ppermute(w_prev, SEQ, to_prev)
-
+    kv_prev, from_next_q, w_from_prev, w_from_next = lax.optimization_barrier(
+        (kv_prev, from_next_q, w_from_prev, w_from_next)
+    )
     adjoint_cols = lax.dynamic_slice_in_dim(adjoint_t, first, COLS, 0).astype(F32)
     values = lax.dynamic_slice_in_dim(layer_t, first, COLS, 0).astype(F32)
     aligned = jnp.sum(adjoint_cols[:, None, :] * expert_out.transpose(2, 1, 0).astype(F32), axis=0)
-    (grads,) = pl.pallas_call(
+    (grads,) = run(
         attend_kernel,
-        in_specs=[SMEM] + [VMEM] * 6,
-        out_specs=[VMEM],
-        **whole([((208, TOK), BF)]),
-        name="attend",
-    )(where, query_t, out_back, kv, kv_prev, from_next_q, aligned)
+        "attend",
+        (where, query_t, out_back, kv, kv_prev, from_next_q, aligned),
+        [((208, TOK), BF)],
+    )
+    gathered, grads, query_cols = lax.optimization_barrier((gathered, grads, query_cols))
     all_grads = lax.all_gather(grads, "exp", axis=0)
-
-    sent, places, _ = pl.pallas_call(
-        dispatch_kernel,
-        in_specs=[VMEM] * 2,
-        out_specs=[VMEM] * 3,
-        **whole([((32, PART + 32, MINE), BF), ((EXPERTS, BLOCKS * TOK), F32), ((EXPERTS, BLOCKS * TOK), F32)]),
-        name="dispatch",
-    )(gathered, query_parts)
-    rows = lax.all_to_all(sent, "exp", 0, 0, tiled=True)
-    (terms,) = pl.pallas_call(
+    (terms,) = run(
         expert_kernel,
-        in_specs=[VMEM] * 8,
-        out_specs=[VMEM],
-        scratch_shapes=[pltpu.VMEM((D + 8, MINE), F32)],
-        **whole([((32, PART, MINE), BF)]),
-        name="expert",
-    )(rows, down, gate, up, own_g, own_u, w_from_prev, w_from_next)
+        "expert",
+        (gathered, down, gate, up, own_g, own_u, w_from_prev, w_from_next),
+        [((32, PART, MINE), BF)],
+        [pltpu.VMEM((D + 8, MINE), F32)],
+        room=32,
+    )
     returned = lax.all_to_all(terms, "exp", 0, 0, tiled=True)
-    (sums,) = pl.pallas_call(
-        combine_kernel,
-        in_specs=[VMEM] * 2,
-        out_specs=[VMEM],
-        **whole([((BLOCKS, PART, TOK), BF)]),
-        name="combine",
-    )(returned, places)
+    (places,) = run(
+        slots_kernel, "slots", (gathered[:, 0:16, D:],), [((EXPERTS, BLOCKS * TOK), F32)]
+    )
+    (sums,) = run(combine_kernel, "combine", (returned, places), [((BLOCKS, PART, TOK), BF)])
     bands = lax.all_to_all(sums, "zh", 0, 0, tiled=True)
 
     pad = ((0, PART - COLS), (0, 0))
     router_cols = jnp.pad(lax.dynamic_slice_in_dim(router_weight, first, COLS, 0), pad)
+    (attended,) = run(
+        project_kernel,
+        "project",
+        (all_grads, query_cols, jnp.pad(key_weight, pad), jnp.pad(value_weight, pad), router_cols, shares, routes_t),
+        [((PART, TOK), F32)],
+    )
     gain = jnp.pad(lax.dynamic_slice_in_dim(norm_gain, first, COLS, 0)[:, None], pad)
     values = jnp.pad(values, pad)
-    (attended,) = pl.pallas_call(
-        project_kernel,
-        in_specs=[VMEM] * 7,
-        out_specs=[VMEM],
-        **whole([((PART, TOK), F32)]),
-        name="project",
-    )(all_grads, rows, jnp.pad(key_weight, pad), jnp.pad(value_weight, pad), router_cols, shares, routes_t)
-    lifted, stat = pl.pallas_call(
-        lift_kernel,
-        in_specs=[VMEM] * 4,
-        out_specs=[VMEM] * 2,
-        **whole([((PART, TOK), F32), ((32, TOK), F32)]),
-        name="lift",
-    )(bands, attended, gain, values)
+    lifted, stat = run(
+        lift_kernel, "lift", (bands, attended, gain, values), [((PART, TOK), F32), ((32, TOK), F32)]
+    )
     stats = lax.all_to_all(stat, "exp", 0, 0, tiled=True)
-    (result,) = pl.pallas_call(
+    (result,) = run(
         finish_kernel,
-        in_specs=[VMEM] * 5,
-        out_specs=[VMEM],
-        **whole([((COLS, TOK), F32)]),
-        name="finish",
-    )(stats, lifted, values, inverse, seed_grad.T + adjoint_cols)
+        "finish",
+        (stats, lifted, values, inverse, seed_grad.T + adjoint_cols),
+        [((COLS, TOK), F32)],
+    )
     return result.T
 
 

time: 197 us -> 168 us (0.85)
  blocking collectives: 34.2 us -> 0 us
  waiting for transfers between devices: 49 us -> 74 us
  local copies, waits for them, and re-layouts: 20.7 us -> 7.24 us
  Pallas kernels: 22.6 us -> 17 us
    all_to_all x1 -> x0, blocking collectives: 34.2 us -> none  [on_device(): returned = lax.all_to_all(terms, 'exp', 0, 0, tiled=True)]
    ppermute x1, waiting for transfers between devices: 1.03 us -> 19.7 us  [on_device(): kv_prev = lax.ppermute(kv, SEQ, to_next)]
    ppermute x1, waiting for transfers between devices: 18 us -> 0.01 us  [on_device(): w_from_prev = lax.ppermute(w_next, SEQ, to_next)]
    all_gather x1, waiting for transfers between devices: 0.02 us -> 15.8 us  [on_device(): all_grads = lax.all_gather(grads, 'exp', axis=0)]
    unnamed x57 -> x37, local copies, waits for them, and re-layouts: 15.8 us -> 3.02 us
    all_to_all x1, waiting for transfers between devices: 11 us -> 0.01 us  [on_device(): bands = lax.all_to_all(sums, 'zh', 0, 0, tiled=True)]
    ppermute x1, waiting for transfers between devices: 0.01 us -> 10.4 us  [on_device(): lax.ppermute(jnp.concatenate([query_t, out_back, kv], axis=0), SEQ, to_prev)]
    all_to_all x2, starting transfers between devices: 28 us -> 17.8 us  [the longest x1 9.72 us: on_device(): returned = lax.all_to_all(terms, 'exp', 0, 0, tiled=True)]
  transfers between devices with their start and end apart: 9 -> 10, of which waited for: 5 -> 5; matrix products, arithmetic and copies ran while one was open for 3% -> 4% of each run, Pallas kernels for 6% -> 7%
where the time goes in v2:
time: 168 us; the launch traced here: 167 us
  waiting for transfers between devices  74 us (44%)
  starting transfers between devices  51.4 us (31%)
  Pallas kernels  17 us (10%)
  between operations  13.7 us (8%)
  local copies, waits for them, and re-layouts  7.24 us (4%)
  other arithmetic  3.09 us (2%)
    all_to_all x1, waiting for transfers between devices, on_device(): returned = lax.all_to_all(terms, 'exp', 0, 0, tiled=True)  22 us
    ppermute x1, waiting for transfers between devices, on_device(): kv_prev = lax.ppermute(kv, SEQ, to_next)  19.7 us
    pallas_call x10, Pallas kernels, run(): pl.pallas_call(kernel, grid=(1,), in_specs=[scalars if a.dtype == jnp.int...  17 us
    all_gather x1, waiting for transfers between devices, on_device(): all_grads = lax.all_gather(grads, 'exp', axis=0)  15.8 us
    ppermute x1, waiting for transfers between devices, on_device(): lax.ppermute(jnp.concatenate([query_t, out_back, kv], axis=0), SEQ, to_prev)  10.4 us
    all_to_all x1, starting transfers between devices, on_device(): returned = lax.all_to_all(terms, 'exp', 0, 0, tiled=True)  9.72 us
    ppermute x1, starting transfers between devices, on_device(): w_from_next = lax.ppermute(w_prev, SEQ, to_prev)  9.5 us
    all_to_all x1, starting transfers between devices, on_device(): query_cols = lax.all_to_all(query_parts, 'exp', 0, 0, tiled=True)  8.04 us
  transfers between devices with their start and end apart: 10, of which 5 were waited for; matrix products, arithmetic and copies ran while one was open for 4% of the time, Pallas kernels for 7%

profile of v2, /device:TPU:1, one launch (start us, length us, event | category | flops | bytes accessed | tf_op | source)
XLA Modules:
  0.0 166.6 jit_solution(17825046920475516349)
XLA Ops:
  6.6 0.7 pad_add_fusion.where
  7.3 3.3 %route.1 = (bf16[32,2944]{1,0:T(8,128)(2,1)}, f32[1,128]{1,0:T(1,128)}, f32[4,128]{1,0:T(4,128)}, bf16[64,128]{1,0:T(8,128)(2,1)}) custom-call(s32[3]{0:T(128)} %pad_add_fusion.where, bf16[2880,128]{1,0:T(8,128)(2,1)} %bitcast.61, f32[2880]{0:T(1024)} %gain.1, bf16[32,2880]{1,0:T(8,128)(2,1)} %bitcast.62, s32[4,128]{1,0:T(4,128)} %bitcast.58, ...), custom_call_target="tpu_custom_call" | custom-call | tf_op jit(solution)/shard_map/route/pallas_call | solution.py:55
  10.6 2.2 %pack.1 = (bf16[160,2880]{1,0:T(8,128)(2,1)}, bf16[160,2880]{1,0:T(8,128)(2,1)}, bf16[96,256]{1,0:T(8,128)(2,1)S(1)}, bf16[96,256]{1,0:T(8,128)(2,1)S(1)}) custom-call(s32[3]{0:T(128)S(1)} %copy-done.11, bf16[96,2880]{1,0:T(8,128)(2,1)S(1)} %bitcast.43, bf16[96,2880]{1,0:T(8,128)(2,1)S(1)} %bitcast.45, bf16[96,2880]{1,0:T(8,128)(2,1)S(1)} %bitcast.47, ...), custom_call_target="tpu_custom_call" | custom-call | tf_op jit(solution)/shard_map/pack/pallas_call | solution.py:55
  12.8 4.5 %collective-permute-start.2 = (bf16[160,2880]{1,0:T(8,128)(2,1)}, bf16[160,2880]{1,0:T(8,128)(2,1)S(1)}, u32[]{:S(2)}, u32[]{:S(2)}) collective-permute-start(bf16[160,2880]{1,0:T(8,128)(2,1)} %get-tuple-element.29), channel_id=1, source_target_pairs={{0,32},{32,64},{64,96},{96,128},{128,160},{160,192},{192,224},{224... | collective-permute-start | bytes 2764808 | tf_op jit(solution)/shard_map/ppermute | solution.py:341
  17.3 9.5 %collective-permute-start.3 = (bf16[160,2880]{1,0:T(8,128)(2,1)}, bf16[160,2880]{1,0:T(8,128)(2,1)}, u32[]{:S(2)}, u32[]{:S(2)}) collective-permute-start(bf16[160,2880]{1,0:T(8,128)(2,1)} %get-tuple-element.30), channel_id=1, source_target_pairs={{32,0},{64,32},{96,64},{128,96},{160,128},{192,160},{224,192},{256... | collective-permute-start | bytes 2764808 | tf_op jit(solution)/shard_map/ppermute | solution.py:342
  26.8 1.1 share.1
  28.0 8.0 %all-to-all-start = ((bf16[32,32,256]{2,1,0:T(8,128)(2,1)}), bf16[32,32,256]{2,1,0:T(8,128)(2,1)S(1)}, u32[]{:S(2)}, u32[]{:S(2)}) async-start(bf16[32,32,256]{2,1,0:T(8,128)(2,1)} %share.1), calls=%async_computation | async-start | bytes 1048576 | tf_op jit(solution)/shard_map/all_to_all | solution.py:345
  36.1 0.9 constant_dynamic-slice_fusion.1
  37.0 1.9 %collective-permute-start = (bf16[128,128]{1,0:T(8,128)(2,1)S(1)}, bf16[128,128]{1,0:T(8,128)(2,1)S(1)}, u32[]{:S(2)}, u32[]{:S(2)}) collective-permute-start(bf16[128,128]{1,0:T(8,128)(2,1)S(1)} %pad_maximum_fusion.kv), channel_id=1, source_target_pairs={{0,32},{32,64},{64,96},{96,128},{128,160},{160,192},{192,224},{224... | collective-permute-start | bytes 98312 | tf_op jit(solution)/shard_map/ppermute | solution.py:351
  39.0 0.7 maximum_maximum_fusion
  39.7 4.6 %collective-permute-start.1 = (bf16[256,128]{1,0:T(8,128)(2,1)}, bf16[256,128]{1,0:T(8,128)(2,1)S(1)}, u32[]{:S(2)}, u32[]{:S(2)}) collective-permute-start(bf16[256,128]{1,0:T(8,128)(2,1)} %maximum_maximum_fusion), channel_id=1, source_target_pairs={{32,0},{64,32},{96,64},{128,96},{160,128},{192,160},{224,192},{256... | collective-permute-start | bytes 196616 | tf_op jit(solution)/shard_map/ppermute | solution.py:352
  44.2 0.8 convert_bitcast_fusion
  45.1 19.7 %collective-permute-done.kv_prev = bf16[128,128]{1,0:T(8,128)(2,1)S(1)} collective-permute-done((bf16[128,128]{1,0:T(8,128)(2,1)S(1)}, bf16[128,128]{1,0:T(8,128)(2,1)S(1)}, u32[]{:S(2)}, u32[]{:S(2)}) %collective-permute-start) | collective-permute-done | bytes 32800 | tf_op jit(solution)/shard_map/ppermute | solution.py:351
  64.8 10.4 %collective-permute-done.1.next_q = bf16[256,128]{1,0:T(8,128)(2,1)S(1)} collective-permute-done((bf16[256,128]{1,0:T(8,128)(2,1)}, bf16[256,128]{1,0:T(8,128)(2,1)S(1)}, u32[]{:S(2)}, u32[]{:S(2)}) %collective-permute-start.1) | collective-permute-done | bytes 65568 | tf_op jit(solution)/shard_map/ppermute | solution.py:352
  75.2 1.6 attend.1
  76.9 1.4 copy-done.4
  78.3 4.8 %expert.1 = bf16[32,96,256]{2,1,0:T(8,128)(2,1)} custom-call(bf16[8,32,2944]{2,1,0:T(8,128)(2,1)S(1)} %bitcast.51, bf16[96,2880]{1,0:T(8,128)(2,1)S(1)} %bitcast.44, bf16[96,2880]{1,0:T(8,128)(2,1)S(1)} %bitcast.46, bf16[96,2880]{1,0:T(8,128)(2,1)S(1)} %bitcast.48, bf16[96,256]{1,0:T(8,128)(2,1)S(1)} %get-tuple-element.35.own_g, ...), custom_call_target="tpu_custom_call" | custom-call | tf_op jit(solution)/shard_map/expert/pallas_call | solution.py:55
  83.0 9.7 %all-to-all-start.1 = ((bf16[32,96,256]{2,1,0:T(8,128)(2,1)}), bf16[32,96,256]{2,1,0:T(8,128)(2,1)S(1)}, u32[]{:S(2)}, u32[]{:S(2)}) async-start(bf16[32,96,256]{2,1,0:T(8,128)(2,1)} %expert.1), calls=%async_computation.1 | async-start | bytes 3145728 | tf_op jit(solution)/shard_map/all_to_all | solution.py:375
  92.8 0.9 slice.3.metas
  93.8 22.0 %all-to-all-done.1.returned = bf16[32,96,256]{2,1,0:T(8,128)(2,1)S(1)} async-done(((bf16[32,96,256]{2,1,0:T(8,128)(2,1)}), bf16[32,96,256]{2,1,0:T(8,128)(2,1)S(1)}, u32[]{:S(2)}, u32[]{:S(2)}) %all-to-all-start.1) | async-done | bytes 1572896 | tf_op jit(solution)/shard_map/all_to_all | solution.py:375
  115.8 1.9 %combine.1 = bf16[8,96,128]{2,1,0:T(8,128)(2,1)} custom-call(bf16[32,96,256]{2,1,0:T(8,128)(2,1)S(1)} %all-to-all-done.1.returned, f32[32,1024]{1,0:T(8,128)S(1)} %slots.1.places), custom_call_target="tpu_custom_call" | custom-call | tf_op jit(solution)/shard_map/combine/pallas_call | solution.py:55
  117.7 7.9 %all-to-all-start.2 = ((bf16[8,96,128]{2,1,0:T(8,128)(2,1)}), bf16[8,96,128]{2,1,0:T(8,128)(2,1)S(1)}, u32[]{:S(2)}, u32[]{:S(2)}) async-start(bf16[8,96,128]{2,1,0:T(8,128)(2,1)} %combine.1), calls=%async_computation.2 | async-start | bytes 393216 | tf_op jit(solution)/shard_map/all_to_all | solution.py:380
  125.6 0.8 constant_dynamic-slice_fusion
  126.6 0.8 dynamic-slice_bitcast_fusion.1
  127.5 0.8 dynamic-slice_bitcast_fusion
  128.3 15.8 %all-gather.7.cloned.1.call-done = bf16[6656,128]{1,0:T(8,128)(2,1)} async-done(((bf16[208,128]{1,0:T(8,128)(2,1)}), bf16[6656,128]{1,0:T(8,128)(2,1)}) %all-gather.7.cloned.1.call-update) | async-done | bytes 1703952 | tf_op jit(solution)/shard_map/all_gather | solution.py:366
  144.1 1.5 copy-done.3
  145.5 0.7 project.1.attended
  146.3 0.7 lift.1
  147.0 5.2 %all-to-all-start.3 = ((f32[32,1,128]{2,1,0:T(1,128)}), f32[32,1,128]{2,1,0:T(1,128)S(1)}, u32[]{:S(2)}, u32[]{:S(2)}) async-start(f32[32,1,128]{2,1,0:T(1,128)} %bitcast.25), calls=%async_computation.3 | async-start | bytes 32768 | tf_op jit(solution)/shard_map/all_to_all | solution.py:395
  152.2 0.8 bitcast_add_fusion.base
  153.0 6.1 %all-to-all-done.3 = f32[32,1,128]{2,1,0:T(1,128)S(1)} async-done(((f32[32,1,128]{2,1,0:T(1,128)}), f32[32,1,128]{2,1,0:T(1,128)S(1)}, u32[]{:S(2)}, u32[]{:S(2)}) %all-to-all-start.3) | async-done | bytes 16416 | tf_op jit(solution)/shard_map/all_to_all | solution.py:395
  (54 shorter events, 1.4 us)
Async XLA Ops:
  6.5 4.0 %copy-start = (bf16[1,96,2880]{2,1,0:T(8,128)(2,1)S(1)}, bf16[1,96,2880]{2,1,0:T(8,128)(2,1)}, u32[]{:S(2)}) copy-start(bf16[1,96,2880]{2,1,0:T(8,128)(2,1)} %param.35) | copy-start | bytes 1658884
  6.5 4.0 %copy-start.1 = (bf16[1,2880,96]{1,2,0:T(8,128)(2,1)S(1)}, bf16[1,2880,96]{1,2,0:T(8,128)(2,1)}, u32[]{:S(2)}) copy-start(bf16[1,2880,96]{1,2,0:T(8,128)(2,1)} %param.33) | copy-start | bytes 1658884
  6.5 4.0 %copy-start.2 = (bf16[1,2880,96]{1,2,0:T(8,128)(2,1)S(1)}, bf16[1,2880,96]{1,2,0:T(8,128)(2,1)}, u32[]{:S(2)}) copy-start(bf16[1,2880,96]{1,2,0:T(8,128)(2,1)} %param.34) | copy-start | bytes 1658884
  6.5 4.0 %copy-start.6 = (bf16[1,512,96]{1,2,0:T(8,128)(2,1)S(1)}, bf16[1,512,96]{1,2,0:T(8,128)(2,1)}, u32[]{:S(2)}) copy-start(bf16[1,512,96]{1,2,0:T(8,128)(2,1)} %param.36) | copy-start | bytes 294916
  6.5 4.1 %copy-start.7 = (bf16[1,512,96]{1,2,0:T(8,128)(2,1)S(1)}, bf16[1,512,96]{1,2,0:T(8,128)(2,1)}, u32[]{:S(2)}) copy-start(bf16[1,512,96]{1,2,0:T(8,128)(2,1)} %param.37) | copy-start | bytes 294916
  6.5 70.3 %all-gather.5.cloned.1.call-start = ((), (), s32[]{:S(2)}) async-start(), calls=%async_computation.4 | async-start | bytes 1695744 | tf_op jit(solution)/shard_map/all_gather | solution.py:329
  7.3 3.3 %copy-start.11 = (s32[3]{0:T(128)S(1)}, s32[3]{0:T(128)}, u32[]{:S(2)}) copy-start(s32[3]{0:T(128)} %pad_add_fusion.where) | copy-start | bytes 40
  7.3 19.5 %copy-start.5 = (bf16[2880,64]{0,1:T(8,128)(2,1)S(1)}, bf16[2880,64]{0,1:T(8,128)(2,1)}, u32[]{:S(2)}) copy-start(bf16[2880,64]{0,1:T(8,128)(2,1)} %param.29) | copy-start | bytes 1105924
  12.8 26.2 %copy-start.8 = (bf16[128,64]{0,1:T(8,128)(2,1)S(1)}, bf16[128,64]{0,1:T(8,128)(2,1)}, u32[]{:S(2)}) copy-start(bf16[128,64]{0,1:T(8,128)(2,1)} %param.26) | copy-start | bytes 49156
  12.8 26.2 %copy-start.9 = (bf16[64,128]{1,0:T(8,128)(2,1)S(1)}, bf16[64,128]{1,0:T(8,128)(2,1)}, u32[]{:S(2)}) copy-start(bf16[64,128]{1,0:T(8,128)(2,1)} %get-tuple-element.26.out_back) | copy-start | bytes 49156
  12.8 32.2 %copy-start.14 = (bf16[128,4,90]{0,1,2:T(4,128)(2,1)S(1)}, bf16[128,4,90]{0,1,2:T(4,128)(2,1)}, u32[]{:S(2)}) copy-start(bf16[128,4,90]{0,1,2:T(4,128)(2,1)} %param.25) | copy-start | bytes 276484
  12.8 62.4 %collective-permute-start.2 = (bf16[160,2880]{1,0:T(8,128)(2,1)}, bf16[160,2880]{1,0:T(8,128)(2,1)S(1)}, u32[]{:S(2)}, u32[]{:S(2)}) collective-permute-start(bf16[160,2880]{1,0:T(8,128)(2,1)} %get-tuple-element.29), channel_id=1, source_target_pairs={{0,32},{32,64},{64,96},{96,128},{128,160},{160,192},{192,224},{224... | collective-permute-start | bytes 2764808 | tf_op jit(solution)/shard_map/ppermute | solution.py:341
  17.3 57.9 %collective-permute-start.3 = (bf16[160,2880]{1,0:T(8,128)(2,1)}, bf16[160,2880]{1,0:T(8,128)(2,1)}, u32[]{:S(2)}, u32[]{:S(2)}) collective-permute-start(bf16[160,2880]{1,0:T(8,128)(2,1)} %get-tuple-element.30), channel_id=1, source_target_pairs={{32,0},{64,32},{96,64},{128,96},{160,128},{192,160},{224,192},{256... | collective-permute-start | bytes 2764808 | tf_op jit(solution)/shard_map/ppermute | solution.py:342
  28.0 48.9 %all-to-all-start = ((bf16[32,32,256]{2,1,0:T(8,128)(2,1)}), bf16[32,32,256]{2,1,0:T(8,128)(2,1)S(1)}, u32[]{:S(2)}, u32[]{:S(2)}) async-start(bf16[32,32,256]{2,1,0:T(8,128)(2,1)} %share.1), calls=%async_computation | async-start | bytes 1048576 | tf_op jit(solution)/shard_map/all_to_all | solution.py:345
  36.0 108.1 %all-gather.7.cloned.1.call-start = ((), (), s32[]{:S(2)}) async-start(), calls=%async_computation.5 | async-start | bytes 1757184 | tf_op jit(solution)/shard_map/all_gather | solution.py:366
  37.0 27.7 %collective-permute-start = (bf16[128,128]{1,0:T(8,128)(2,1)S(1)}, bf16[128,128]{1,0:T(8,128)(2,1)S(1)}, u32[]{:S(2)}, u32[]{:S(2)}) collective-permute-start(bf16[128,128]{1,0:T(8,128)(2,1)S(1)} %pad_maximum_fusion.kv), channel_id=1, source_target_pairs={{0,32},{32,64},{64,96},{96,128},{128,160},{160,192},{192,224},{224... | collective-permute-start | bytes 98312 | tf_op jit(solution)/shard_map/ppermute | solution.py:351
  39.7 35.5 %collective-permute-start.1 = (bf16[256,128]{1,0:T(8,128)(2,1)}, bf16[256,128]{1,0:T(8,128)(2,1)S(1)}, u32[]{:S(2)}, u32[]{:S(2)}) collective-permute-start(bf16[256,128]{1,0:T(8,128)(2,1)} %maximum_maximum_fusion), channel_id=1, source_target_pairs={{32,0},{64,32},{96,64},{128,96},{160,128},{192,160},{224,192},{256... | collective-permute-start | bytes 196616 | tf_op jit(solution)/shard_map/ppermute | solution.py:352
  76.9 1.4 copy-start.4
  83.0 32.7 %all-to-all-start.1 = ((bf16[32,96,256]{2,1,0:T(8,128)(2,1)}), bf16[32,96,256]{2,1,0:T(8,128)(2,1)S(1)}, u32[]{:S(2)}, u32[]{:S(2)}) async-start(bf16[32,96,256]{2,1,0:T(8,128)(2,1)} %expert.1), calls=%async_computation.1 | async-start | bytes 3145728 | tf_op jit(solution)/shard_map/all_to_all | solution.py:375
  92.8 32.8 %copy-start.15 = (bf16[90,256]{1,0:T(8,128)(2,1)S(1)}, bf16[90,256]{1,0:T(8,128)(2,1)}, u32[]{:S(2)}) copy-start(bf16[90,256]{1,0:T(8,128)(2,1)} %param.30) | copy-start | bytes 138244
  92.8 32.8 %copy-start.16 = (bf16[90,256]{1,0:T(8,128)(2,1)S(1)}, bf16[90,256]{1,0:T(8,128)(2,1)}, u32[]{:S(2)}) copy-start(bf16[90,256]{1,0:T(8,128)(2,1)} %param.31) | copy-start | bytes 138244
  92.8 51.3 %copy-start.10 = (s32[128,4]{0,1:T(4,128)S(1)}, s32[128,4]{0,1:T(4,128)}, u32[]{:S(2)}) copy-start(s32[128,4]{0,1:T(4,128)} %param.24) | copy-start | bytes 6148
  92.8 51.3 %copy-start.12 = (f32[4,128]{1,0:T(4,128)S(1)}, f32[4,128]{1,0:T(4,128)}, u32[]{:S(2)}) copy-start(f32[4,128]{1,0:T(4,128)} %get-tuple-element.41.shares) | copy-start | bytes 6148
  117.7 28.6 %all-to-all-start.2 = ((bf16[8,96,128]{2,1,0:T(8,128)(2,1)}), bf16[8,96,128]{2,1,0:T(8,128)(2,1)S(1)}, u32[]{:S(2)}, u32[]{:S(2)}) async-start(bf16[8,96,128]{2,1,0:T(8,128)(2,1)} %combine.1), calls=%async_computation.2 | async-start | bytes 393216 | tf_op jit(solution)/shard_map/all_to_all | solution.py:380
  126.4 25.8 %copy-start.17 = (f32[128,90]{0,1:T(8,128)S(1)}, f32[128,90]{0,1:T(8,128)}, u32[]{:S(2)}) copy-start(f32[128,90]{0,1:T(8,128)} %param.20) | copy-start | bytes 138244
  127.5 31.6 %copy-start.13 = (f32[1,128]{1,0:T(1,128)S(1)}, f32[1,128]{1,0:T(1,128)}, u32[]{:S(2)}) copy-start(f32[1,128]{1,0:T(1,128)} %get-tuple-element.44.inverse) | copy-start | bytes 1540
  144.1 1.5 copy-start.3
  147.0 12.1 %all-to-all-start.3 = ((f32[32,1,128]{2,1,0:T(1,128)}), f32[32,1,128]{2,1,0:T(1,128)S(1)}, u32[]{:S(2)}, u32[]{:S(2)}) async-start(f32[32,1,128]{2,1,0:T(1,128)} %bitcast.25), calls=%async_computation.3 | async-start | bytes 32768 | tf_op jit(solution)/shard_map/all_to_all | solution.py:395
Sparse Core Ops, SparseCore 0:
  10.7 66.0 all-gather.4
  80.0 64.0 all-gather.6

commit v3 on v2

--- a/solution.py
+++ b/solution.py
@@ -142,7 +142,7 @@
                 ref[3 * HALF :, lane : lane + MINE] = sent[first + 16 * m : first + 16 * m + 16, :]
 
 
-def attend_kernel(where, query, out_back, kv, kv_prev, next_q, aligned, grads):
+def attend_kernel(where, query, out_back, kv, kv_prev, next_q, grads):
     block = where[2]
     key_at, query_at = rows_of((TOK, TOK)), lanes_of((TOK, TOK))
     same = key_at <= query_at
@@ -182,16 +182,9 @@
         (dot(q, sb_own, across) + live * dot(q_next, sb_next, across)) * SCALE
     ).astype(BF)
     grads[128:192, :] = (dot(out, p_own, across) + live * dot(out_next, p_next, across)).astype(BF)
-    line = rows_of((16, TOK))
-    tail = jnp.zeros((16, TOK), F32)
-    for k in range(TOPK):
-        high = aligned[k : k + 1, :].astype(BF).astype(F32)
-        tail = jnp.where(line == k, high, tail)
-        tail = jnp.where(line == TOPK + k, aligned[k : k + 1, :] - high, tail)
-    grads[192:208, :] = tail.astype(BF)
-
-
-def expert_kernel(rows, down, gate, up, own_g, own_u, from_prev, from_next, sent, total):
+
+
+def expert_kernel(rows, down, gate, up, own_g, own_u, from_prev, from_next, aligned, sent, total):
     features = rows[:, :, 0:D].reshape(MINE, D)
     across = ((1,), (1,))
 
@@ -218,11 +211,17 @@
         jnp.concatenate(weights, axis=0), jnp.concatenate(backs, axis=0), ((0,), (0,))
     )
     total[D:, :] = jnp.zeros((8, MINE), F32)
+    line = rows_of((PART, MINE))
+    tail = jnp.zeros((PART, MINE), F32)
+    for k in range(TOPK):
+        value = aligned[k : k + 1, :]
+        high = value.astype(BF).astype(F32)
+        tail = jnp.where(line == COLS + k, jnp.concatenate([high, value - high], axis=1), tail)
     for c in range(32):
-        sent[c, :, :] = total[c * COLS : c * COLS + PART, :].astype(BF)
-
-
-def combine_kernel(returned, places, sent):
+        sent[c, :, :] = jnp.where(line < COLS, total[c * COLS : c * COLS + PART, :], tail).astype(BF)
+
+
+def combine_kernel(returned, places, sent, aligned):
     slot = rows_of((CAP, TOK)).astype(F32)
     empty = jnp.zeros((CAP, TOK), BF)
     for h in range(2):
@@ -238,9 +237,14 @@
             total = total + dot(jnp.concatenate(terms, axis=1), jnp.concatenate(picks, axis=0))
         for b in range(4):
             sent[4 * h + b, :, :] = total[:, b * TOK : (b + 1) * TOK].astype(BF)
-
-
-def project_kernel(grads, rows, key_w, value_w, router, shares, routes, attended):
+    tail = jnp.zeros((16, MINE), F32)
+    for e in range(EXPERTS):
+        tail = tail + returned[e, PART - 16 :, :].astype(F32)
+    first = COLS - (PART - 16)
+    aligned[...] = tail[first : first + TOPK, 0:TOK] + tail[first : first + TOPK, TOK:]
+
+
+def project_kernel(grads, rows, key_w, value_w, router, shares, routes, sums, attended):
     total = jnp.zeros((PART, TOK), F32)
     for h in range(QH):
         for n in range(2):
@@ -248,18 +252,15 @@
             total = total + dot(weight, grads[h, 32 * n : 32 * n + 32, :], ((0,), (0,)))
     group = QH // KVH
     for first, weight in ((64, key_w), (128, value_w)):
-        sums = []
+        groups = []
         for g in range(KVH):
             some = grads[g * group, first : first + 64, :].astype(F32)
             for h in range(g * group + 1, (g + 1) * group):
                 some = some + grads[h, first : first + 64, :].astype(F32)
-            sums.append(some)
-        high, low = split(jnp.concatenate(sums, axis=0))
+            groups.append(some)
+        high, low = split(jnp.concatenate(groups, axis=0))
         total = total + dot(weight[...], high) + dot(weight[...], low)
-    tail = grads[0, 192:208, :].astype(F32)
-    for h in range(1, QH):
-        tail = tail + grads[h, 192:208, :].astype(F32)
-    aligned = [tail[k : k + 1, :] + tail[TOPK + k : TOPK + k + 1, :] for k in range(TOPK)]
+    aligned = [sums[k : k + 1, :] for k in range(TOPK)]
     mean = sum(shares[k : k + 1, :] * aligned[k] for k in range(TOPK))
     names = rows_of((EXPERTS, TOK))
     coef = jnp.zeros((EXPERTS, TOK), F32)
@@ -350,24 +351,24 @@
     query_t = stored_query.T
     kv_prev = lax.ppermute(kv, SEQ, to_next)
     from_next_q = lax.ppermute(jnp.concatenate([query_t, out_back, kv], axis=0), SEQ, to_prev)
-    kv_prev, from_next_q, w_from_prev, w_from_next = lax.optimization_barrier(
-        (kv_prev, from_next_q, w_from_prev, w_from_next)
-    )
     adjoint_cols = lax.dynamic_slice_in_dim(adjoint_t, first, COLS, 0).astype(F32)
     values = lax.dynamic_slice_in_dim(layer_t, first, COLS, 0).astype(F32)
     aligned = jnp.sum(adjoint_cols[:, None, :] * expert_out.transpose(2, 1, 0).astype(F32), axis=0)
+    kv_prev, from_next_q, w_from_prev, w_from_next, aligned = lax.optimization_barrier(
+        (kv_prev, from_next_q, w_from_prev, w_from_next, aligned)
+    )
     (grads,) = run(
         attend_kernel,
         "attend",
-        (where, query_t, out_back, kv, kv_prev, from_next_q, aligned),
-        [((208, TOK), BF)],
+        (where, query_t, out_back, kv, kv_prev, from_next_q),
+        [((192, TOK), BF)],
     )
     gathered, grads, query_cols = lax.optimization_barrier((gathered, grads, query_cols))
     all_grads = lax.all_gather(grads, "exp", axis=0)
     (terms,) = run(
         expert_kernel,
         "expert",
-        (gathered, down, gate, up, own_g, own_u, w_from_prev, w_from_next),
+        (gathered, down, gate, up, own_g, own_u, w_from_prev, w_from_next, aligned),
         [((32, PART, MINE), BF)],
         [pltpu.VMEM((D + 8, MINE), F32)],
         room=32,
@@ -376,7 +377,12 @@
     (places,) = run(
         slots_kernel, "slots", (gathered[:, 0:16, D:],), [((EXPERTS, BLOCKS * TOK), F32)]
     )
-    (sums,) = run(combine_kernel, "combine", (returned, places), [((BLOCKS, PART, TOK), BF)])
+    sums, aligned_sums = run(
+        combine_kernel,
+        "combine",
+        (returned, places),
+        [((BLOCKS, PART, TOK), BF), ((TOPK, TOK), F32)],
+    )
     bands = lax.all_to_all(sums, "zh", 0, 0, tiled=True)
 
     pad = ((0, PART - COLS), (0, 0))
@@ -384,7 +390,7 @@
     (attended,) = run(
         project_kernel,
         "project",
-        (all_grads, query_cols, jnp.pad(key_weight, pad), jnp.pad(value_weight, pad), router_cols, shares, routes_t),
+        (all_grads, query_cols, jnp.pad(key_weight, pad), jnp.pad(value_weight, pad), router_cols, shares, routes_t, aligned_sums),
         [((PART, TOK), F32)],
     )
     gain = jnp.pad(lax.dynamic_slice_in_dim(norm_gain, first, COLS, 0)[:, None], pad)

time: 168 us -> 167 us (level)
  no operation moved by 1% of the time
where the time goes in v3:
time: 167 us; the launch traced here: 166 us
  waiting for transfers between devices  74.6 us (45%)
  starting transfers between devices  50.6 us (30%)
  Pallas kernels  17 us (10%)
  between operations  13.8 us (8%)
  local copies, waits for them, and re-layouts  7.18 us (4%)
  other arithmetic  3.02 us (2%)
    all_to_all x1, waiting for transfers between devices, on_device(): returned = lax.all_to_all(terms, 'exp', 0, 0, tiled=True)  21.8 us
    ppermute x1, waiting for transfers between devices, on_device(): kv_prev = lax.ppermute(kv, SEQ, to_next)  20.7 us
    pallas_call x10, Pallas kernels, run(): pl.pallas_call(kernel, grid=(1,), in_specs=[scalars if a.dtype == jnp.int...  17 us
    all_gather x1, waiting for transfers between devices, on_device(): all_grads = lax.all_gather(grads, 'exp', axis=0)  15.7 us
    ppermute x1, waiting for transfers between devices, on_device(): lax.ppermute(jnp.concatenate([query_t, out_back, kv], axis=0), SEQ, to_prev)  10.2 us
    all_to_all x1, starting transfers between devices, on_device(): returned = lax.all_to_all(terms, 'exp', 0, 0, tiled=True)  9.81 us
    ppermute x1, starting transfers between devices, on_device(): w_from_next = lax.ppermute(w_prev, SEQ, to_prev)  9.5 us
    all_to_all x1, starting transfers between devices, on_device(): query_cols = lax.all_to_all(query_parts, 'exp', 0, 0, tiled=True)  8.04 us
  transfers between devices with their start and end apart: 10, of which 5 were waited for; matrix products, arithmetic and copies ran while one was open for 4% of the time, Pallas kernels for 7%

profile of v3, /device:TPU:1, one launch (start us, length us, event | category | flops | bytes accessed | tf_op | source)
XLA Modules:
  0.0 166.2 jit_solution(16203358183514413724)
XLA Ops:
  7.2 3.3 %route.1 = (bf16[32,2944]{1,0:T(8,128)(2,1)}, f32[1,128]{1,0:T(1,128)}, f32[4,128]{1,0:T(4,128)}, bf16[64,128]{1,0:T(8,128)(2,1)}) custom-call(s32[3]{0:T(128)} %pad_add_fusion.where, bf16[2880,128]{1,0:T(8,128)(2,1)} %bitcast.61, f32[2880]{0:T(1024)} %gain.1, bf16[32,2880]{1,0:T(8,128)(2,1)} %bitcast.62, s32[4,128]{1,0:T(4,128)} %bitcast.58, ...), custom_call_target="tpu_custom_call" | custom-call | tf_op jit(solution)/shard_map/route/pallas_call | solution.py:55
  10.6 2.2 %pack.1 = (bf16[160,2880]{1,0:T(8,128)(2,1)}, bf16[160,2880]{1,0:T(8,128)(2,1)}, bf16[96,256]{1,0:T(8,128)(2,1)S(1)}, bf16[96,256]{1,0:T(8,128)(2,1)S(1)}) custom-call(s32[3]{0:T(128)S(1)} %copy-done.11, bf16[96,2880]{1,0:T(8,128)(2,1)S(1)} %bitcast.43, bf16[96,2880]{1,0:T(8,128)(2,1)S(1)} %bitcast.45, bf16[96,2880]{1,0:T(8,128)(2,1)S(1)} %bitcast.47, ...), custom_call_target="tpu_custom_call" | custom-call | tf_op jit(solution)/shard_map/pack/pallas_call | solution.py:55
  12.8 4.5 %collective-permute-start.2 = (bf16[160,2880]{1,0:T(8,128)(2,1)}, bf16[160,2880]{1,0:T(8,128)(2,1)S(1)}, u32[]{:S(2)}, u32[]{:S(2)}) collective-permute-start(bf16[160,2880]{1,0:T(8,128)(2,1)} %get-tuple-element.32), channel_id=1, source_target_pairs={{0,32},{32,64},{64,96},{96,128},{128,160},{160,192},{192,224},{224... | collective-permute-start | bytes 2764808 | tf_op jit(solution)/shard_map/ppermute | solution.py:342
  17.3 9.5 %collective-permute-start.3 = (bf16[160,2880]{1,0:T(8,128)(2,1)}, bf16[160,2880]{1,0:T(8,128)(2,1)}, u32[]{:S(2)}, u32[]{:S(2)}) collective-permute-start(bf16[160,2880]{1,0:T(8,128)(2,1)} %get-tuple-element.33), channel_id=1, source_target_pairs={{32,0},{64,32},{96,64},{128,96},{160,128},{192,160},{224,192},{256... | collective-permute-start | bytes 2764808 | tf_op jit(solution)/shard_map/ppermute | solution.py:343
  26.8 1.1 share.1
  27.9 8.0 %all-to-all-start = ((bf16[32,32,256]{2,1,0:T(8,128)(2,1)}), bf16[32,32,256]{2,1,0:T(8,128)(2,1)S(1)}, u32[]{:S(2)}, u32[]{:S(2)}) async-start(bf16[32,32,256]{2,1,0:T(8,128)(2,1)} %share.1), calls=%async_computation | async-start | bytes 1048576 | tf_op jit(solution)/shard_map/all_to_all | solution.py:346
  36.1 0.8 constant_dynamic-slice_fusion.1
  36.9 0.7 maximum_maximum_fusion
  37.6 3.6 %collective-permute-start.1 = (bf16[256,128]{1,0:T(8,128)(2,1)}, bf16[256,128]{1,0:T(8,128)(2,1)S(1)}, u32[]{:S(2)}, u32[]{:S(2)}) collective-permute-start(bf16[256,128]{1,0:T(8,128)(2,1)} %maximum_maximum_fusion), channel_id=1, source_target_pairs={{32,0},{64,32},{96,64},{128,96},{160,128},{192,160},{224,192},{256... | collective-permute-start | bytes 196616 | tf_op jit(solution)/shard_map/ppermute | solution.py:353
  41.4 1.9 %collective-permute-start = (bf16[128,128]{1,0:T(8,128)(2,1)S(1)}, bf16[128,128]{1,0:T(8,128)(2,1)S(1)}, u32[]{:S(2)}, u32[]{:S(2)}) collective-permute-start(bf16[128,128]{1,0:T(8,128)(2,1)S(1)} %pad_maximum_fusion.kv), channel_id=1, source_target_pairs={{0,32},{32,64},{64,96},{96,128},{128,160},{160,192},{192,224},{224... | collective-permute-start | bytes 98312 | tf_op jit(solution)/shard_map/ppermute | solution.py:352
  43.3 0.8 convert_bitcast_fusion
  44.2 20.7 %collective-permute-done.kv_prev = bf16[128,128]{1,0:T(8,128)(2,1)S(1)} collective-permute-done((bf16[128,128]{1,0:T(8,128)(2,1)S(1)}, bf16[128,128]{1,0:T(8,128)(2,1)S(1)}, u32[]{:S(2)}, u32[]{:S(2)}) %collective-permute-start) | collective-permute-done | bytes 32800 | tf_op jit(solution)/shard_map/ppermute | solution.py:352
  64.9 10.2 %collective-permute-done.1.next_q = bf16[256,128]{1,0:T(8,128)(2,1)S(1)} collective-permute-done((bf16[256,128]{1,0:T(8,128)(2,1)}, bf16[256,128]{1,0:T(8,128)(2,1)S(1)}, u32[]{:S(2)}, u32[]{:S(2)}) %collective-permute-start.1) | collective-permute-done | bytes 65568 | tf_op jit(solution)/shard_map/ppermute | solution.py:353
  75.1 1.6 attend.1
  76.8 1.4 copy-done.3
  78.2 4.7 %expert.1 = bf16[32,96,256]{2,1,0:T(8,128)(2,1)} custom-call(bf16[8,32,2944]{2,1,0:T(8,128)(2,1)S(1)} %bitcast.50, bf16[96,2880]{1,0:T(8,128)(2,1)S(1)} %bitcast.44, bf16[96,2880]{1,0:T(8,128)(2,1)S(1)} %bitcast.46, bf16[96,2880]{1,0:T(8,128)(2,1)S(1)} %bitcast.48, bf16[96,256]{1,0:T(8,128)(2,1)S(1)} %get-tuple-element.38.own_g, ...), custom_call_target="tpu_custom_call" | custom-call | tf_op jit(solution)/shard_map/expert/pallas_call | solution.py:55
  82.9 9.8 %all-to-all-start.1 = ((bf16[32,96,256]{2,1,0:T(8,128)(2,1)}), bf16[32,96,256]{2,1,0:T(8,128)(2,1)S(1)}, u32[]{:S(2)}, u32[]{:S(2)}) async-start(bf16[32,96,256]{2,1,0:T(8,128)(2,1)} %expert.1), calls=%async_computation.1 | async-start | bytes 3145728 | tf_op jit(solution)/shard_map/all_to_all | solution.py:376
  92.8 0.9 slice.3.metas
  93.8 21.8 %all-to-all-done.1.returned = bf16[32,96,256]{2,1,0:T(8,128)(2,1)S(1)} async-done(((bf16[32,96,256]{2,1,0:T(8,128)(2,1)}), bf16[32,96,256]{2,1,0:T(8,128)(2,1)S(1)}, u32[]{:S(2)}, u32[]{:S(2)}) %all-to-all-start.1) | async-done | bytes 1572896 | tf_op jit(solution)/shard_map/all_to_all | solution.py:376
  115.6 1.9 %combine.1 = (bf16[8,96,128]{2,1,0:T(8,128)(2,1)}, f32[4,128]{1,0:T(4,128)S(1)}) custom-call(bf16[32,96,256]{2,1,0:T(8,128)(2,1)S(1)} %all-to-all-done.1.returned, f32[32,1024]{1,0:T(8,128)S(1)} %slots.1.places), custom_call_target="tpu_custom_call" | custom-call | tf_op jit(solution)/shard_map/combine/pallas_call | solution.py:55
  117.5 8.0 %all-to-all-start.2 = ((bf16[8,96,128]{2,1,0:T(8,128)(2,1)}), bf16[8,96,128]{2,1,0:T(8,128)(2,1)S(1)}, u32[]{:S(2)}, u32[]{:S(2)}) async-start(bf16[8,96,128]{2,1,0:T(8,128)(2,1)} %get-tuple-element.43), calls=%async_computation.2 | async-start | bytes 393216 | tf_op jit(solution)/shard_map/all_to_all | solution.py:386
  125.4 0.8 constant_dynamic-slice_fusion
  126.4 0.8 dynamic-slice_bitcast_fusion.1
  127.4 0.8 dynamic-slice_bitcast_fusion
  128.1 15.7 %all-gather.7.cloned.1.call-done = bf16[6144,128]{1,0:T(8,128)(2,1)} async-done(((bf16[192,128]{1,0:T(8,128)(2,1)}), bf16[6144,128]{1,0:T(8,128)(2,1)}) %all-gather.7.cloned.1.call-update) | async-done | bytes 1572880 | tf_op jit(solution)/shard_map/all_gather | solution.py:367
  143.8 1.4 copy-done.4
  145.2 0.7 project.1.attended
  146.0 0.7 lift.1
  146.7 5.2 %all-to-all-start.3 = ((f32[32,1,128]{2,1,0:T(1,128)}), f32[32,1,128]{2,1,0:T(1,128)S(1)}, u32[]{:S(2)}, u32[]{:S(2)}) async-start(f32[32,1,128]{2,1,0:T(1,128)} %bitcast.25), calls=%async_computation.3 | async-start | bytes 32768 | tf_op jit(solution)/shard_map/all_to_all | solution.py:401
  151.9 0.8 bitcast_add_fusion.base
  152.7 6.1 %all-to-all-done.3 = f32[32,1,128]{2,1,0:T(1,128)S(1)} async-done(((f32[32,1,128]{2,1,0:T(1,128)}), f32[32,1,128]{2,1,0:T(1,128)S(1)}, u32[]{:S(2)}, u32[]{:S(2)}) %all-to-all-start.3) | async-done | bytes 16416 | tf_op jit(solution)/shard_map/all_to_all | solution.py:401
  158.7 0.6 finish.1
  (56 shorter events, 1.4 us)
Async XLA Ops:
  6.5 3.9 %copy-start.1 = (bf16[1,2880,96]{1,2,0:T(8,128)(2,1)S(1)}, bf16[1,2880,96]{1,2,0:T(8,128)(2,1)}, u32[]{:S(2)}) copy-start(bf16[1,2880,96]{1,2,0:T(8,128)(2,1)} %param.33) | copy-start | bytes 1658884
  6.5 4.0 %copy-start.2 = (bf16[1,2880,96]{1,2,0:T(8,128)(2,1)S(1)}, bf16[1,2880,96]{1,2,0:T(8,128)(2,1)}, u32[]{:S(2)}) copy-start(bf16[1,2880,96]{1,2,0:T(8,128)(2,1)} %param.34) | copy-start | bytes 1658884
  6.5 4.0 %copy-start = (bf16[1,96,2880]{2,1,0:T(8,128)(2,1)S(1)}, bf16[1,96,2880]{2,1,0:T(8,128)(2,1)}, u32[]{:S(2)}) copy-start(bf16[1,96,2880]{2,1,0:T(8,128)(2,1)} %param.35) | copy-start | bytes 1658884
  6.5 4.0 %copy-start.6 = (bf16[1,512,96]{1,2,0:T(8,128)(2,1)S(1)}, bf16[1,512,96]{1,2,0:T(8,128)(2,1)}, u32[]{:S(2)}) copy-start(bf16[1,512,96]{1,2,0:T(8,128)(2,1)} %param.36) | copy-start | bytes 294916
  6.5 4.0 %copy-start.7 = (bf16[1,512,96]{1,2,0:T(8,128)(2,1)S(1)}, bf16[1,512,96]{1,2,0:T(8,128)(2,1)}, u32[]{:S(2)}) copy-start(bf16[1,512,96]{1,2,0:T(8,128)(2,1)} %param.37) | copy-start | bytes 294916
  6.5 70.2 %all-gather.5.cloned.1.call-start = ((), (), s32[]{:S(2)}) async-start(), calls=%async_computation.4 | async-start | bytes 1695744 | tf_op jit(solution)/shard_map/all_gather | solution.py:330
  7.2 3.3 %copy-start.11 = (s32[3]{0:T(128)S(1)}, s32[3]{0:T(128)}, u32[]{:S(2)}) copy-start(s32[3]{0:T(128)} %pad_add_fusion.where) | copy-start | bytes 40
  7.2 19.6 %copy-start.5 = (bf16[2880,64]{0,1:T(8,128)(2,1)S(1)}, bf16[2880,64]{0,1:T(8,128)(2,1)}, u32[]{:S(2)}) copy-start(bf16[2880,64]{0,1:T(8,128)(2,1)} %param.29) | copy-start | bytes 1105924
  10.5 25.5 %copy-start.18 = (bf16[128,256]{1,0:T(8,128)(2,1)S(1)}, bf16[128,256]{1,0:T(8,128)(2,1)}, u32[]{:S(2)}) copy-start(bf16[128,256]{1,0:T(8,128)(2,1)} %param.28) | copy-start | bytes 196612
  10.6 26.4 %copy-start.8 = (bf16[128,64]{0,1:T(8,128)(2,1)S(1)}, bf16[128,64]{0,1:T(8,128)(2,1)}, u32[]{:S(2)}) copy-start(bf16[128,64]{0,1:T(8,128)(2,1)} %param.26) | copy-start | bytes 49156
  10.6 26.4 %copy-start.9 = (bf16[64,128]{1,0:T(8,128)(2,1)S(1)}, bf16[64,128]{1,0:T(8,128)(2,1)}, u32[]{:S(2)}) copy-start(bf16[64,128]{1,0:T(8,128)(2,1)} %get-tuple-element.29.out_back) | copy-start | bytes 49156
  12.8 31.3 %copy-start.14 = (bf16[128,4,90]{0,1,2:T(4,128)(2,1)S(1)}, bf16[128,4,90]{0,1,2:T(4,128)(2,1)}, u32[]{:S(2)}) copy-start(bf16[128,4,90]{0,1,2:T(4,128)(2,1)} %param.25) | copy-start | bytes 276484
  12.8 62.3 %collective-permute-start.2 = (bf16[160,2880]{1,0:T(8,128)(2,1)}, bf16[160,2880]{1,0:T(8,128)(2,1)S(1)}, u32[]{:S(2)}, u32[]{:S(2)}) collective-permute-start(bf16[160,2880]{1,0:T(8,128)(2,1)} %get-tuple-element.32), channel_id=1, source_target_pairs={{0,32},{32,64},{64,96},{96,128},{128,160},{160,192},{192,224},{224... | collective-permute-start | bytes 2764808 | tf_op jit(solution)/shard_map/ppermute | solution.py:342
  17.3 57.8 %collective-permute-start.3 = (bf16[160,2880]{1,0:T(8,128)(2,1)}, bf16[160,2880]{1,0:T(8,128)(2,1)}, u32[]{:S(2)}, u32[]{:S(2)}) collective-permute-start(bf16[160,2880]{1,0:T(8,128)(2,1)} %get-tuple-element.33), channel_id=1, source_target_pairs={{32,0},{64,32},{96,64},{128,96},{160,128},{192,160},{224,192},{256... | collective-permute-start | bytes 2764808 | tf_op jit(solution)/shard_map/ppermute | solution.py:343
  27.9 48.8 %all-to-all-start = ((bf16[32,32,256]{2,1,0:T(8,128)(2,1)}), bf16[32,32,256]{2,1,0:T(8,128)(2,1)S(1)}, u32[]{:S(2)}, u32[]{:S(2)}) async-start(bf16[32,32,256]{2,1,0:T(8,128)(2,1)} %share.1), calls=%async_computation | async-start | bytes 1048576 | tf_op jit(solution)/shard_map/all_to_all | solution.py:346
  36.0 107.8 %all-gather.7.cloned.1.call-start = ((), (), s32[]{:S(2)}) async-start(), calls=%async_computation.5 | async-start | bytes 1622016 | tf_op jit(solution)/shard_map/all_gather | solution.py:367
  37.6 37.5 %collective-permute-start.1 = (bf16[256,128]{1,0:T(8,128)(2,1)}, bf16[256,128]{1,0:T(8,128)(2,1)S(1)}, u32[]{:S(2)}, u32[]{:S(2)}) collective-permute-start(bf16[256,128]{1,0:T(8,128)(2,1)} %maximum_maximum_fusion), channel_id=1, source_target_pairs={{32,0},{64,32},{96,64},{128,96},{160,128},{192,160},{224,192},{256... | collective-permute-start | bytes 196616 | tf_op jit(solution)/shard_map/ppermute | solution.py:353
  41.4 23.5 %collective-permute-start = (bf16[128,128]{1,0:T(8,128)(2,1)S(1)}, bf16[128,128]{1,0:T(8,128)(2,1)S(1)}, u32[]{:S(2)}, u32[]{:S(2)}) collective-permute-start(bf16[128,128]{1,0:T(8,128)(2,1)S(1)} %pad_maximum_fusion.kv), channel_id=1, source_target_pairs={{0,32},{32,64},{64,96},{96,128},{128,160},{160,192},{192,224},{224... | collective-permute-start | bytes 98312 | tf_op jit(solution)/shard_map/ppermute | solution.py:352
  76.8 1.4 copy-start.3
  82.9 32.7 %all-to-all-start.1 = ((bf16[32,96,256]{2,1,0:T(8,128)(2,1)}), bf16[32,96,256]{2,1,0:T(8,128)(2,1)S(1)}, u32[]{:S(2)}, u32[]{:S(2)}) async-start(bf16[32,96,256]{2,1,0:T(8,128)(2,1)} %expert.1), calls=%async_computation.1 | async-start | bytes 3145728 | tf_op jit(solution)/shard_map/all_to_all | solution.py:376
  92.7 33.6 %copy-start.15 = (bf16[90,256]{1,0:T(8,128)(2,1)S(1)}, bf16[90,256]{1,0:T(8,128)(2,1)}, u32[]{:S(2)}) copy-start(bf16[90,256]{1,0:T(8,128)(2,1)} %param.30) | copy-start | bytes 138244
  92.8 33.7 %copy-start.16 = (bf16[90,256]{1,0:T(8,128)(2,1)S(1)}, bf16[90,256]{1,0:T(8,128)(2,1)}, u32[]{:S(2)}) copy-start(bf16[90,256]{1,0:T(8,128)(2,1)} %param.31) | copy-start | bytes 138244
  92.8 51.1 %copy-start.10 = (s32[128,4]{0,1:T(4,128)S(1)}, s32[128,4]{0,1:T(4,128)}, u32[]{:S(2)}) copy-start(s32[128,4]{0,1:T(4,128)} %param.24) | copy-start | bytes 6148
  92.8 51.0 %copy-start.12 = (f32[4,128]{1,0:T(4,128)S(1)}, f32[4,128]{1,0:T(4,128)}, u32[]{:S(2)}) copy-start(f32[4,128]{1,0:T(4,128)} %get-tuple-element.46.shares) | copy-start | bytes 6148
  117.5 28.5 %all-to-all-start.2 = ((bf16[8,96,128]{2,1,0:T(8,128)(2,1)}), bf16[8,96,128]{2,1,0:T(8,128)(2,1)S(1)}, u32[]{:S(2)}, u32[]{:S(2)}) async-start(bf16[8,96,128]{2,1,0:T(8,128)(2,1)} %get-tuple-element.43), calls=%async_computation.2 | async-start | bytes 393216 | tf_op jit(solution)/shard_map/all_to_all | solution.py:386
  126.4 25.5 %copy-start.17 = (f32[128,90]{0,1:T(8,128)S(1)}, f32[128,90]{0,1:T(8,128)}, u32[]{:S(2)}) copy-start(f32[128,90]{0,1:T(8,128)} %param.20) | copy-start | bytes 138244
  126.4 32.3 %copy-start.13 = (f32[1,128]{1,0:T(1,128)S(1)}, f32[1,128]{1,0:T(1,128)}, u32[]{:S(2)}) copy-start(f32[1,128]{1,0:T(1,128)} %get-tuple-element.50.inverse) | copy-start | bytes 1540
  143.8 1.4 copy-start.4
  146.7 12.1 %all-to-all-start.3 = ((f32[32,1,128]{2,1,0:T(1,128)}), f32[32,1,128]{2,1,0:T(1,128)S(1)}, u32[]{:S(2)}, u32[]{:S(2)}) async-start(f32[32,1,128]{2,1,0:T(1,128)} %bitcast.25), calls=%async_computation.3 | async-start | bytes 32768 | tf_op jit(solution)/shard_map/all_to_all | solution.py:401
Sparse Core Ops, SparseCore 0:
  10.6 66.1 all-gather.4
  79.9 63.8 all-gather.6

commit v4 on v2

--- a/solution.py
+++ b/solution.py
@@ -69,7 +69,8 @@
     inv = lax.rsqrt(jnp.sum(values * values, axis=0, keepdims=True) / D + EPSILON)
     inverse[...] = inv
     high, low = split(router[...].astype(F32) * gain[...].reshape(1, D))
-    logits = (dot(high, layer[...]) + dot(low, layer[...])) * inv
+    both = dot(jnp.concatenate([high, low], axis=0), layer[...])
+    logits = (both[0:EXPERTS] + both[EXPERTS:]) * inv
     names = rows_of((EXPERTS, TOK))
     picked = [names == routes[k : k + 1, :] for k in range(TOPK)]
     raised = [

time: 168 us -> 168 us (level)
  no operation moved by 1% of the time
where the time goes in v4:
time: 168 us; the launch traced here: 167 us
  waiting for transfers between devices  74 us (44%)
  starting transfers between devices  51.4 us (31%)
  Pallas kernels  17.1 us (10%)
  between operations  13.7 us (8%)
  local copies, waits for them, and re-layouts  7.24 us (4%)
  other arithmetic  3.09 us (2%)
    all_to_all x1, waiting for transfers between devices, on_device(): returned = lax.all_to_all(terms, 'exp', 0, 0, tiled=True)  22 us
    ppermute x1, waiting for transfers between devices, on_device(): kv_prev = lax.ppermute(kv, SEQ, to_next)  19.6 us
    pallas_call x10, Pallas kernels, run(): pl.pallas_call(kernel, grid=(1,), in_specs=[scalars if a.dtype == jnp.int...  17.1 us
    all_gather x1, waiting for transfers between devices, on_device(): all_grads = lax.all_gather(grads, 'exp', axis=0)  15.8 us
    ppermute x1, waiting for transfers between devices, on_device(): lax.ppermute(jnp.concatenate([query_t, out_back, kv], axis=0), SEQ, to_prev)  10.5 us
    all_to_all x1, starting transfers between devices, on_device(): returned = lax.all_to_all(terms, 'exp', 0, 0, tiled=True)  9.73 us
    ppermute x1, starting transfers between devices, on_device(): w_from_next = lax.ppermute(w_prev, SEQ, to_prev)  9.5 us
    all_to_all x1, starting transfers between devices, on_device(): query_cols = lax.all_to_all(query_parts, 'exp', 0, 0, tiled=True)  8.04 us
  transfers between devices with their start and end apart: 10, of which 5 were waited for; matrix products, arithmetic and copies ran while one was open for 4% of the time, Pallas kernels for 7%

profile of v4, /device:TPU:1, one launch (start us, length us, event | category | flops | bytes accessed | tf_op | source)
XLA Modules:
  0.0 166.6 jit_solution(8196278376254637217)
XLA Ops:
  6.6 0.7 pad_add_fusion.where
  7.3 3.3 %route.1 = (bf16[32,2944]{1,0:T(8,128)(2,1)}, f32[1,128]{1,0:T(1,128)}, f32[4,128]{1,0:T(4,128)}, bf16[64,128]{1,0:T(8,128)(2,1)}) custom-call(s32[3]{0:T(128)} %pad_add_fusion.where, bf16[2880,128]{1,0:T(8,128)(2,1)} %bitcast.61, f32[2880]{0:T(1024)} %gain.1, bf16[32,2880]{1,0:T(8,128)(2,1)} %bitcast.62, s32[4,128]{1,0:T(4,128)} %bitcast.58, ...), custom_call_target="tpu_custom_call" | custom-call | tf_op jit(solution)/shard_map/route/pallas_call | solution.py:55
  10.7 2.2 %pack.1 = (bf16[160,2880]{1,0:T(8,128)(2,1)}, bf16[160,2880]{1,0:T(8,128)(2,1)}, bf16[96,256]{1,0:T(8,128)(2,1)S(1)}, bf16[96,256]{1,0:T(8,128)(2,1)S(1)}) custom-call(s32[3]{0:T(128)S(1)} %copy-done.11, bf16[96,2880]{1,0:T(8,128)(2,1)S(1)} %bitcast.43, bf16[96,2880]{1,0:T(8,128)(2,1)S(1)} %bitcast.45, bf16[96,2880]{1,0:T(8,128)(2,1)S(1)} %bitcast.47, ...), custom_call_target="tpu_custom_call" | custom-call | tf_op jit(solution)/shard_map/pack/pallas_call | solution.py:55
  12.8 4.5 %collective-permute-start.2 = (bf16[160,2880]{1,0:T(8,128)(2,1)}, bf16[160,2880]{1,0:T(8,128)(2,1)S(1)}, u32[]{:S(2)}, u32[]{:S(2)}) collective-permute-start(bf16[160,2880]{1,0:T(8,128)(2,1)} %get-tuple-element.29), channel_id=1, source_target_pairs={{0,32},{32,64},{64,96},{96,128},{128,160},{160,192},{192,224},{224... | collective-permute-start | bytes 2764808 | tf_op jit(solution)/shard_map/ppermute | solution.py:342
  17.3 9.5 %collective-permute-start.3 = (bf16[160,2880]{1,0:T(8,128)(2,1)}, bf16[160,2880]{1,0:T(8,128)(2,1)}, u32[]{:S(2)}, u32[]{:S(2)}) collective-permute-start(bf16[160,2880]{1,0:T(8,128)(2,1)} %get-tuple-element.30), channel_id=1, source_target_pairs={{32,0},{64,32},{96,64},{128,96},{160,128},{192,160},{224,192},{256... | collective-permute-start | bytes 2764808 | tf_op jit(solution)/shard_map/ppermute | solution.py:343
  26.9 1.1 share.1
  28.0 8.0 %all-to-all-start = ((bf16[32,32,256]{2,1,0:T(8,128)(2,1)}), bf16[32,32,256]{2,1,0:T(8,128)(2,1)S(1)}, u32[]{:S(2)}, u32[]{:S(2)}) async-start(bf16[32,32,256]{2,1,0:T(8,128)(2,1)} %share.1), calls=%async_computation | async-start | bytes 1048576 | tf_op jit(solution)/shard_map/all_to_all | solution.py:346
  36.1 0.9 constant_dynamic-slice_fusion.1
  37.1 1.9 %collective-permute-start = (bf16[128,128]{1,0:T(8,128)(2,1)S(1)}, bf16[128,128]{1,0:T(8,128)(2,1)S(1)}, u32[]{:S(2)}, u32[]{:S(2)}) collective-permute-start(bf16[128,128]{1,0:T(8,128)(2,1)S(1)} %pad_maximum_fusion.kv), channel_id=1, source_target_pairs={{0,32},{32,64},{64,96},{96,128},{128,160},{160,192},{192,224},{224... | collective-permute-start | bytes 98312 | tf_op jit(solution)/shard_map/ppermute | solution.py:352
  39.0 0.7 maximum_maximum_fusion
  39.7 4.6 %collective-permute-start.1 = (bf16[256,128]{1,0:T(8,128)(2,1)}, bf16[256,128]{1,0:T(8,128)(2,1)S(1)}, u32[]{:S(2)}, u32[]{:S(2)}) collective-permute-start(bf16[256,128]{1,0:T(8,128)(2,1)} %maximum_maximum_fusion), channel_id=1, source_target_pairs={{32,0},{64,32},{96,64},{128,96},{160,128},{192,160},{224,192},{256... | collective-permute-start | bytes 196616 | tf_op jit(solution)/shard_map/ppermute | solution.py:353
  44.3 0.8 convert_bitcast_fusion
  45.2 19.6 %collective-permute-done.kv_prev = bf16[128,128]{1,0:T(8,128)(2,1)S(1)} collective-permute-done((bf16[128,128]{1,0:T(8,128)(2,1)S(1)}, bf16[128,128]{1,0:T(8,128)(2,1)S(1)}, u32[]{:S(2)}, u32[]{:S(2)}) %collective-permute-start) | collective-permute-done | bytes 32800 | tf_op jit(solution)/shard_map/ppermute | solution.py:352
  64.8 10.5 %collective-permute-done.1.next_q = bf16[256,128]{1,0:T(8,128)(2,1)S(1)} collective-permute-done((bf16[256,128]{1,0:T(8,128)(2,1)}, bf16[256,128]{1,0:T(8,128)(2,1)S(1)}, u32[]{:S(2)}, u32[]{:S(2)}) %collective-permute-start.1) | collective-permute-done | bytes 65568 | tf_op jit(solution)/shard_map/ppermute | solution.py:353
  75.3 1.6 attend.1
  77.0 1.4 copy-done.4
  78.3 4.8 %expert.1 = bf16[32,96,256]{2,1,0:T(8,128)(2,1)} custom-call(bf16[8,32,2944]{2,1,0:T(8,128)(2,1)S(1)} %bitcast.51, bf16[96,2880]{1,0:T(8,128)(2,1)S(1)} %bitcast.44, bf16[96,2880]{1,0:T(8,128)(2,1)S(1)} %bitcast.46, bf16[96,2880]{1,0:T(8,128)(2,1)S(1)} %bitcast.48, bf16[96,256]{1,0:T(8,128)(2,1)S(1)} %get-tuple-element.35.own_g, ...), custom_call_target="tpu_custom_call" | custom-call | tf_op jit(solution)/shard_map/expert/pallas_call | solution.py:55
  83.1 9.7 %all-to-all-start.1 = ((bf16[32,96,256]{2,1,0:T(8,128)(2,1)}), bf16[32,96,256]{2,1,0:T(8,128)(2,1)S(1)}, u32[]{:S(2)}, u32[]{:S(2)}) async-start(bf16[32,96,256]{2,1,0:T(8,128)(2,1)} %expert.1), calls=%async_computation.1 | async-start | bytes 3145728 | tf_op jit(solution)/shard_map/all_to_all | solution.py:376
  92.9 0.9 slice.3.metas
  93.9 22.0 %all-to-all-done.1.returned = bf16[32,96,256]{2,1,0:T(8,128)(2,1)S(1)} async-done(((bf16[32,96,256]{2,1,0:T(8,128)(2,1)}), bf16[32,96,256]{2,1,0:T(8,128)(2,1)S(1)}, u32[]{:S(2)}, u32[]{:S(2)}) %all-to-all-start.1) | async-done | bytes 1572896 | tf_op jit(solution)/shard_map/all_to_all | solution.py:376
  115.8 1.9 %combine.1 = bf16[8,96,128]{2,1,0:T(8,128)(2,1)} custom-call(bf16[32,96,256]{2,1,0:T(8,128)(2,1)S(1)} %all-to-all-done.1.returned, f32[32,1024]{1,0:T(8,128)S(1)} %slots.1.places), custom_call_target="tpu_custom_call" | custom-call | tf_op jit(solution)/shard_map/combine/pallas_call | solution.py:55
  117.7 7.9 %all-to-all-start.2 = ((bf16[8,96,128]{2,1,0:T(8,128)(2,1)}), bf16[8,96,128]{2,1,0:T(8,128)(2,1)S(1)}, u32[]{:S(2)}, u32[]{:S(2)}) async-start(bf16[8,96,128]{2,1,0:T(8,128)(2,1)} %combine.1), calls=%async_computation.2 | async-start | bytes 393216 | tf_op jit(solution)/shard_map/all_to_all | solution.py:381
  125.7 0.8 constant_dynamic-slice_fusion
  126.6 0.8 dynamic-slice_bitcast_fusion.1
  127.5 0.8 dynamic-slice_bitcast_fusion
  128.3 15.8 %all-gather.7.cloned.1.call-done = bf16[6656,128]{1,0:T(8,128)(2,1)} async-done(((bf16[208,128]{1,0:T(8,128)(2,1)}), bf16[6656,128]{1,0:T(8,128)(2,1)}) %all-gather.7.cloned.1.call-update) | async-done | bytes 1703952 | tf_op jit(solution)/shard_map/all_gather | solution.py:367
  144.1 1.5 copy-done.3
  145.6 0.7 project.1.attended
  146.4 0.7 lift.1
  147.1 5.2 %all-to-all-start.3 = ((f32[32,1,128]{2,1,0:T(1,128)}), f32[32,1,128]{2,1,0:T(1,128)S(1)}, u32[]{:S(2)}, u32[]{:S(2)}) async-start(f32[32,1,128]{2,1,0:T(1,128)} %bitcast.25), calls=%async_computation.3 | async-start | bytes 32768 | tf_op jit(solution)/shard_map/all_to_all | solution.py:396
  152.3 0.8 bitcast_add_fusion.base
  153.0 6.1 %all-to-all-done.3 = f32[32,1,128]{2,1,0:T(1,128)S(1)} async-done(((f32[32,1,128]{2,1,0:T(1,128)}), f32[32,1,128]{2,1,0:T(1,128)S(1)}, u32[]{:S(2)}, u32[]{:S(2)}) %all-to-all-start.3) | async-done | bytes 16416 | tf_op jit(solution)/shard_map/all_to_all | solution.py:396
  (54 shorter events, 1.4 us)
Async XLA Ops:
  6.5 4.1 %copy-start = (bf16[1,96,2880]{2,1,0:T(8,128)(2,1)S(1)}, bf16[1,96,2880]{2,1,0:T(8,128)(2,1)}, u32[]{:S(2)}) copy-start(bf16[1,96,2880]{2,1,0:T(8,128)(2,1)} %param.35) | copy-start | bytes 1658884
  6.5 4.1 %copy-start.1 = (bf16[1,2880,96]{1,2,0:T(8,128)(2,1)S(1)}, bf16[1,2880,96]{1,2,0:T(8,128)(2,1)}, u32[]{:S(2)}) copy-start(bf16[1,2880,96]{1,2,0:T(8,128)(2,1)} %param.33) | copy-start | bytes 1658884
  6.5 4.1 %copy-start.2 = (bf16[1,2880,96]{1,2,0:T(8,128)(2,1)S(1)}, bf16[1,2880,96]{1,2,0:T(8,128)(2,1)}, u32[]{:S(2)}) copy-start(bf16[1,2880,96]{1,2,0:T(8,128)(2,1)} %param.34) | copy-start | bytes 1658884
  6.5 4.1 %copy-start.6 = (bf16[1,512,96]{1,2,0:T(8,128)(2,1)S(1)}, bf16[1,512,96]{1,2,0:T(8,128)(2,1)}, u32[]{:S(2)}) copy-start(bf16[1,512,96]{1,2,0:T(8,128)(2,1)} %param.36) | copy-start | bytes 294916
  6.5 4.1 %copy-start.7 = (bf16[1,512,96]{1,2,0:T(8,128)(2,1)S(1)}, bf16[1,512,96]{1,2,0:T(8,128)(2,1)}, u32[]{:S(2)}) copy-start(bf16[1,512,96]{1,2,0:T(8,128)(2,1)} %param.37) | copy-start | bytes 294916
  6.5 70.4 %all-gather.5.cloned.1.call-start = ((), (), s32[]{:S(2)}) async-start(), calls=%async_computation.4 | async-start | bytes 1695744 | tf_op jit(solution)/shard_map/all_gather | solution.py:330
  7.3 3.4 %copy-start.11 = (s32[3]{0:T(128)S(1)}, s32[3]{0:T(128)}, u32[]{:S(2)}) copy-start(s32[3]{0:T(128)} %pad_add_fusion.where) | copy-start | bytes 40
  7.3 19.6 %copy-start.5 = (bf16[2880,64]{0,1:T(8,128)(2,1)S(1)}, bf16[2880,64]{0,1:T(8,128)(2,1)}, u32[]{:S(2)}) copy-start(bf16[2880,64]{0,1:T(8,128)(2,1)} %param.29) | copy-start | bytes 1105924
  12.8 26.2 %copy-start.8 = (bf16[128,64]{0,1:T(8,128)(2,1)S(1)}, bf16[128,64]{0,1:T(8,128)(2,1)}, u32[]{:S(2)}) copy-start(bf16[128,64]{0,1:T(8,128)(2,1)} %param.26) | copy-start | bytes 49156
  12.8 26.2 %copy-start.9 = (bf16[64,128]{1,0:T(8,128)(2,1)S(1)}, bf16[64,128]{1,0:T(8,128)(2,1)}, u32[]{:S(2)}) copy-start(bf16[64,128]{1,0:T(8,128)(2,1)} %get-tuple-element.26.out_back) | copy-start | bytes 49156
  12.8 32.2 %copy-start.14 = (bf16[128,4,90]{0,1,2:T(4,128)(2,1)S(1)}, bf16[128,4,90]{0,1,2:T(4,128)(2,1)}, u32[]{:S(2)}) copy-start(bf16[128,4,90]{0,1,2:T(4,128)(2,1)} %param.25) | copy-start | bytes 276484
  12.8 62.4 %collective-permute-start.2 = (bf16[160,2880]{1,0:T(8,128)(2,1)}, bf16[160,2880]{1,0:T(8,128)(2,1)S(1)}, u32[]{:S(2)}, u32[]{:S(2)}) collective-permute-start(bf16[160,2880]{1,0:T(8,128)(2,1)} %get-tuple-element.29), channel_id=1, source_target_pairs={{0,32},{32,64},{64,96},{96,128},{128,160},{160,192},{192,224},{224... | collective-permute-start | bytes 2764808 | tf_op jit(solution)/shard_map/ppermute | solution.py:342
  17.3 57.9 %collective-permute-start.3 = (bf16[160,2880]{1,0:T(8,128)(2,1)}, bf16[160,2880]{1,0:T(8,128)(2,1)}, u32[]{:S(2)}, u32[]{:S(2)}) collective-permute-start(bf16[160,2880]{1,0:T(8,128)(2,1)} %get-tuple-element.30), channel_id=1, source_target_pairs={{32,0},{64,32},{96,64},{128,96},{160,128},{192,160},{224,192},{256... | collective-permute-start | bytes 2764808 | tf_op jit(solution)/shard_map/ppermute | solution.py:343
  28.0 48.9 %all-to-all-start = ((bf16[32,32,256]{2,1,0:T(8,128)(2,1)}), bf16[32,32,256]{2,1,0:T(8,128)(2,1)S(1)}, u32[]{:S(2)}, u32[]{:S(2)}) async-start(bf16[32,32,256]{2,1,0:T(8,128)(2,1)} %share.1), calls=%async_computation | async-start | bytes 1048576 | tf_op jit(solution)/shard_map/all_to_all | solution.py:346
  36.1 108.1 %all-gather.7.cloned.1.call-start = ((), (), s32[]{:S(2)}) async-start(), calls=%async_computation.5 | async-start | bytes 1757184 | tf_op jit(solution)/shard_map/all_gather | solution.py:367
  37.1 27.7 %collective-permute-start = (bf16[128,128]{1,0:T(8,128)(2,1)S(1)}, bf16[128,128]{1,0:T(8,128)(2,1)S(1)}, u32[]{:S(2)}, u32[]{:S(2)}) collective-permute-start(bf16[128,128]{1,0:T(8,128)(2,1)S(1)} %pad_maximum_fusion.kv), channel_id=1, source_target_pairs={{0,32},{32,64},{64,96},{96,128},{128,160},{160,192},{192,224},{224... | collective-permute-start | bytes 98312 | tf_op jit(solution)/shard_map/ppermute | solution.py:352
  39.7 35.5 %collective-permute-start.1 = (bf16[256,128]{1,0:T(8,128)(2,1)}, bf16[256,128]{1,0:T(8,128)(2,1)S(1)}, u32[]{:S(2)}, u32[]{:S(2)}) collective-permute-start(bf16[256,128]{1,0:T(8,128)(2,1)} %maximum_maximum_fusion), channel_id=1, source_target_pairs={{32,0},{64,32},{96,64},{128,96},{160,128},{192,160},{224,192},{256... | collective-permute-start | bytes 196616 | tf_op jit(solution)/shard_map/ppermute | solution.py:353
  76.9 1.4 copy-start.4
  83.1 32.7 %all-to-all-start.1 = ((bf16[32,96,256]{2,1,0:T(8,128)(2,1)}), bf16[32,96,256]{2,1,0:T(8,128)(2,1)S(1)}, u32[]{:S(2)}, u32[]{:S(2)}) async-start(bf16[32,96,256]{2,1,0:T(8,128)(2,1)} %expert.1), calls=%async_computation.1 | async-start | bytes 3145728 | tf_op jit(solution)/shard_map/all_to_all | solution.py:376
  92.8 32.8 %copy-start.15 = (bf16[90,256]{1,0:T(8,128)(2,1)S(1)}, bf16[90,256]{1,0:T(8,128)(2,1)}, u32[]{:S(2)}) copy-start(bf16[90,256]{1,0:T(8,128)(2,1)} %param.30) | copy-start | bytes 138244
  92.9 32.8 %copy-start.16 = (bf16[90,256]{1,0:T(8,128)(2,1)S(1)}, bf16[90,256]{1,0:T(8,128)(2,1)}, u32[]{:S(2)}) copy-start(bf16[90,256]{1,0:T(8,128)(2,1)} %param.31) | copy-start | bytes 138244
  92.9 51.3 %copy-start.10 = (s32[128,4]{0,1:T(4,128)S(1)}, s32[128,4]{0,1:T(4,128)}, u32[]{:S(2)}) copy-start(s32[128,4]{0,1:T(4,128)} %param.24) | copy-start | bytes 6148
  92.9 51.3 %copy-start.12 = (f32[4,128]{1,0:T(4,128)S(1)}, f32[4,128]{1,0:T(4,128)}, u32[]{:S(2)}) copy-start(f32[4,128]{1,0:T(4,128)} %get-tuple-element.41.shares) | copy-start | bytes 6148
  117.7 28.6 %all-to-all-start.2 = ((bf16[8,96,128]{2,1,0:T(8,128)(2,1)}), bf16[8,96,128]{2,1,0:T(8,128)(2,1)S(1)}, u32[]{:S(2)}, u32[]{:S(2)}) async-start(bf16[8,96,128]{2,1,0:T(8,128)(2,1)} %combine.1), calls=%async_computation.2 | async-start | bytes 393216 | tf_op jit(solution)/shard_map/all_to_all | solution.py:381
  126.5 25.8 %copy-start.17 = (f32[128,90]{0,1:T(8,128)S(1)}, f32[128,90]{0,1:T(8,128)}, u32[]{:S(2)}) copy-start(f32[128,90]{0,1:T(8,128)} %param.20) | copy-start | bytes 138244
  127.5 31.6 %copy-start.13 = (f32[1,128]{1,0:T(1,128)S(1)}, f32[1,128]{1,0:T(1,128)}, u32[]{:S(2)}) copy-start(f32[1,128]{1,0:T(1,128)} %get-tuple-element.44.inverse) | copy-start | bytes 1540
  144.1 1.5 copy-start.3
  147.1 12.1 %all-to-all-start.3 = ((f32[32,1,128]{2,1,0:T(1,128)}), f32[32,1,128]{2,1,0:T(1,128)S(1)}, u32[]{:S(2)}, u32[]{:S(2)}) async-start(f32[32,1,128]{2,1,0:T(1,128)} %bitcast.25), calls=%async_computation.3 | async-start | bytes 32768 | tf_op jit(solution)/shard_map/all_to_all | solution.py:396
Sparse Core Ops, SparseCore 0:
  10.7 66.1 all-gather.4
  80.1 64.0 all-gather.6
